TPU v7x, 128 devices: a whole 4x4x4 slice. The times are simulated.
128 devices in a mesh: gy: 16 (over x, z_lo, core), gz: 8 (over y, z_hi).
Axes of the slice: x: 4, y: 4, z: 4 (z_hi: 2, z_lo: 2; z = z_hi * 2 + z_lo), core: 2. Of those that a mesh axis runs over, the one named last changes fastest.
Arguments:
- velocity: float32 [3, 128, 512, 1024], P(None, None, 'gy', 'gz'), may hold values from -8 to 8
- wall_mask: int32 [512, 1024], P('gy', 'gz'), may hold values 0 or 1
- hartmann_mask: int32 [512, 1024], P('gy', 'gz'), may hold values 0 or 1
- tile_table: int32 [8, 32, 64], P(None, 'gy', 'gz'), may hold values from 0 to 127, as said below
- w_in: bfloat16 [256, 24], replicated, may hold values from -1.25 to 1.25
- b_in: float32 [256], replicated, may hold values from -3 to 3
- w_mid: bfloat16 [256, 256], replicated, may hold values from -0.375 to 0.375
- b_mid: float32 [256], replicated, may hold values from -3 to 3
- w_out: bfloat16 [6, 256], replicated, may hold values from -0.375 to 0.375
- b_out: float32 [6], replicated, may hold values from -3 to 3
Outputs:
- stepped: bfloat16 [3, 128, 512, 1024], P(None, None, 'gy', 'gz')
- prediction: float32 [6, 1048576], P(None, ('gy', 'gz'))
- loss: float32 [], replicated
- grad_w_in: float32 [256, 24], replicated
- grad_b_in: float32 [256], replicated
- grad_w_mid: float32 [256, 256], replicated
- grad_b_mid: float32 [256], replicated
- grad_w_out: float32 [6, 256], replicated
- grad_b_out: float32 [6], replicated
Inputs may be any that keep to these rules, and one draw needn't show every extreme that they name: `tile_table`: within the tiles of one device's block of the table every slot number appears exactly once.
All inputs are finite; a program needn't handle non-finite values. No bound on the sum of `wall_mask` or of `hartmann_mask` on one device may be relied on, other than what follows from the above.
Results may differ from a plain program's by a relative error of at most 0.0021.
Values may be sent and summed in bfloat16 or wider, within the bound.
A program may use at most 192 MiB of HBM per device.

v0:
```python
import jax
import jax.numpy as jnp
from jax import lax
from jax.sharding import PartitionSpec as P

STATIONS = 128
TILE = 16
BLOCK = 4
PTS = 64


time_step = 0.2
viscosity = 0.5
stuart_number = 1.0
stress_pairs = ((0, 0), (1, 1), (2, 2), (0, 1), (0, 2), (1, 2))
contract_rows = (((1,), (1,)), ((), ()))
contract_cols = (((0,), (0,)), ((), ()))


def extended(cells, sides, width):
    for axis, dim in sides:
        count = lax.axis_size(axis)
        ends = count - 1
        head = lax.slice_in_dim(cells, 0, width, axis=dim)
        tail = lax.slice_in_dim(cells, cells.shape[dim] - width, cells.shape[dim], axis=dim)
        cells = jnp.concatenate(
            [
                lax.ppermute(tail, axis, [(i, (i + 1) % count) for i in range(ends)]),
                cells,
                lax.ppermute(head, axis, [((i + 1) % count, i) for i in range(ends)]),
            ],
            axis=dim,
        )
    return cells


def pool_tables():
    cells = TILE**3
    points_edge = TILE // BLOCK
    half_block = BLOCK // 2
    index = jnp.arange(cells, dtype=jnp.int32)
    along_x = index // (TILE * TILE)
    along_y = index // TILE % TILE
    along_z = index % TILE
    point = (
        along_x // BLOCK * points_edge * points_edge
        + along_y // BLOCK * points_edge
        + along_z // BLOCK
    )
    quarter = (
        along_x % BLOCK // half_block * 4
        + along_y % BLOCK // half_block * 2
        + along_z % BLOCK // half_block
    )
    column = quarter * PTS + point
    sub_pool = (
        (column[:, None] == jnp.arange(PTS * 8, dtype=jnp.int32)[None, :]).astype(jnp.float32)
        / float(half_block**3)
    ).astype(jnp.bfloat16)
    point_pool = (point[:, None] == jnp.arange(PTS, dtype=jnp.int32)[None, :]).astype(
        jnp.float32
    ) / float(BLOCK**3)
    return (sub_pool, point_pool)


def assemble(tile_rows):
    tile_count = tile_rows.shape[0]
    cells = TILE**3
    sub_pool, point_pool = pool_tables()
    sub_means = jnp.dot(
        tile_rows.reshape(tile_count * 3, cells), sub_pool, preferred_element_type=jnp.float32
    )
    sub_means = sub_means.reshape(tile_count, 3, 8, PTS)
    inputs = sub_means.transpose(1, 2, 0, 3).reshape(24, tile_count * PTS)
    point_means = jnp.mean(sub_means, axis=2)
    values = tile_rows.reshape(tile_count, 3, cells).astype(jnp.float32)
    stresses = []
    for left_comp, right_comp in stress_pairs:
        product = jnp.dot(
            values[:, left_comp] * values[:, right_comp],
            point_pool,
            precision=lax.Precision.HIGHEST,
        )
        stresses.append(product - point_means[:, left_comp] * point_means[:, right_comp])
    targets = jnp.stack(stresses).reshape(6, tile_count * PTS)
    return jnp.concatenate([inputs, targets], axis=0).astype(jnp.bfloat16)


def silu_slope(value):
    sigma = jax.nn.sigmoid(value)
    return sigma * (1.0 + value * (1.0 - sigma))


def cut_tiles(stepped):
    height = stepped.shape[3]
    width = stepped.shape[2]
    groups = height // TILE
    cell_index = jnp.arange(height, dtype=jnp.int32)[:, None, None]
    target = (
        jnp.arange(groups, dtype=jnp.int32)[None, :, None] * TILE
        + jnp.arange(TILE, dtype=jnp.int32)[None, None, :]
    )
    selector = (cell_index == target).astype(jnp.bfloat16)
    moved = jnp.einsum(
        "csyz,zkt->kcsyt", stepped, selector, preferred_element_type=jnp.float32
    ).astype(jnp.bfloat16)
    moved = moved.reshape(groups, 3, STATIONS // TILE, TILE, width // TILE, TILE, TILE)
    return moved.transpose(2, 4, 0, 1, 3, 5, 6).reshape(-1, 3 * TILE**3)


def on_device(
    velocity, wall_mask, hartmann_mask, tile_table, w_in, b_in, w_mid, b_mid, w_out, b_out
):
    fluid = (1 - wall_mask).astype(jnp.float32)
    masked = velocity * fluid[None, None]
    padded = extended(masked, (("gy", 2), ("gz", 3)), 1)
    north_face = padded[:, :, 2:, 1:-1]
    south_face = padded[:, :, :-2, 1:-1]
    upper_face = padded[:, :, 1:-1, 2:]
    lower_face = padded[:, :, 1:-1, :-2]
    ahead_plane = jnp.roll(masked, -1, axis=1)
    behind = jnp.roll(masked, 1, axis=1)
    laplace = (
        ahead_plane + behind + north_face + south_face + upper_face + lower_face - 6.0 * masked
    )
    advect = (
        masked[0] * ((ahead_plane - behind) * 0.5)
        + masked[1] * ((north_face - south_face) * 0.5)
        + masked[2] * ((upper_face - lower_face) * 0.5)
    )
    factor = stuart_number * (1.0 + hartmann_mask.astype(jnp.float32))
    lorentz = jnp.concatenate([-factor * masked[:2], jnp.zeros_like(masked[2:])], axis=0)
    stepped = ((masked + time_step * (viscosity * laplace - advect + lorentz)) * fluid).astype(
        jnp.bfloat16
    )
    tile_rows = cut_tiles(stepped)
    slot_order = tile_table.reshape(-1)
    ordered = jnp.zeros_like(tile_rows).at[slot_order].set(tile_rows)
    arrived = lax.all_to_all(ordered, ("gy", "gz"), split_axis=0, concat_axis=0, tiled=True)
    packed = assemble(arrived)
    samples_total = packed.shape[1] * lax.axis_size("gy") * lax.axis_size("gz")
    scale = 2.0 / (6 * samples_total)
    inputs = packed[:24]
    targets = packed[24:].astype(jnp.float32)
    first_pre = jnp.dot(w_in, inputs, preferred_element_type=jnp.float32) + b_in[:, None]
    first_act = jax.nn.silu(first_pre).astype(jnp.bfloat16)
    second_pre = jnp.dot(w_mid, first_act, preferred_element_type=jnp.float32) + b_mid[:, None]
    second_act = jax.nn.silu(second_pre).astype(jnp.bfloat16)
    prediction = jnp.dot(w_out, second_act, preferred_element_type=jnp.float32) + b_out[:, None]
    residual = prediction - targets
    squares = jnp.sum(residual * residual)
    pred_grad = (residual * scale).astype(jnp.bfloat16)
    grad_w_out = lax.dot_general(
        pred_grad, second_act, contract_rows, preferred_element_type=jnp.float32
    )
    grad_b_out = jnp.sum(pred_grad.astype(jnp.float32), axis=1)
    second_grad = (
        lax.dot_general(w_out, pred_grad, contract_cols, preferred_element_type=jnp.float32)
        * silu_slope(second_pre)
    ).astype(jnp.bfloat16)
    grad_w_mid = lax.dot_general(
        second_grad, first_act, contract_rows, preferred_element_type=jnp.float32
    )
    grad_b_mid = jnp.sum(second_grad.astype(jnp.float32), axis=1)
    first_grad = (
        lax.dot_general(w_mid, second_grad, contract_cols, preferred_element_type=jnp.float32)
        * silu_slope(first_pre)
    ).astype(jnp.bfloat16)
    grad_w_in = lax.dot_general(
        first_grad, inputs, contract_rows, preferred_element_type=jnp.float32
    )
    grad_b_in = jnp.sum(first_grad.astype(jnp.float32), axis=1)
    grad_w_in, grad_b_in, grad_w_mid, grad_b_mid, grad_w_out, grad_b_out, squares = lax.psum(
        (grad_w_in, grad_b_in, grad_w_mid, grad_b_mid, grad_w_out, grad_b_out, squares),
        ("gy", "gz"),
    )
    loss = squares / (6 * samples_total)
    return (
        stepped,
        prediction,
        loss,
        grad_w_in,
        grad_b_in,
        grad_w_mid,
        grad_b_mid,
        grad_w_out,
        grad_b_out,
    )


def solution(mesh):
    in_specs = (
        P(None, None, "gy", "gz"),
        P("gy", "gz"),
        P("gy", "gz"),
        P(None, "gy", "gz"),
        P(),
        P(),
        P(),
        P(),
        P(),
        P(),
    )
    out_specs = (
        P(None, None, "gy", "gz"),
        P(None, ("gy", "gz")),
        P(),
        P(),
        P(),
        P(),
        P(),
        P(),
        P(),
    )
    return jax.shard_map(
        on_device, mesh=mesh, in_specs=in_specs, out_specs=out_specs, check_vma=False
    )
```

profile of v0, /device:TPU:1, one launch (start us, length us, event | category | flops | bytes accessed | tf_op | source)
XLA Modules:
  0.0 525.5 jit_solution(12944520825112583255)
XLA Ops:
  7.9 6.4 %copy_multiply_fusion = f32[3,128,32,128]{3,1,2,0:T(8,128)S(1)} fusion(f32[3,128,32,128]{3,2,1,0:T(8,128)} %param.10, f32[32,128]{1,0:T(8,128)S(1)} %subtract_convert_fusion), kind=kLoop, calls=%fused_computation.31 | loop fusion | flops 1572864 | bytes 12599296 | tf_op jit(solution)/shard_map/mul | solution.py:115
  18.6 3.5 collective-permute-start.1
  25.0 6.3 %fusion.191 = (f32[3,127,32,128]{3,1,2,0:T(8,128)}, f32[3,127,32,128]{3,1,2,0:T(8,128)}) fusion(f32[3,128,32,128]{3,1,2,0:T(8,128)S(1)} %copy_multiply_fusion), kind=kLoop, calls=%fused_computation.225 | loop fusion | bytes 24969216 | tf_op jit(solution)/shard_map/jit(_roll_static)/slice | solution.py:121
  35.2 6.5 %pad_maximum_fusion = f32[3,128,34,128]{3,1,2,0:T(8,128)} fusion(f32[3,128,1,128]{3,1,2,0:T(8,128)S(1)} %collective-permute-done, f32[3,128,32,128]{3,1,2,0:T(8,128)} %copy-done.1, f32[3,128,1,128]{3,1,2,0:T(8,128)} %collective-permute-done.1), kind=kLoop, calls=%fused_computation.20 | loop fusion | flops 3342336 | bytes 13369344 | tf_op jit(solution)/shard_map/concatenate | solution.py:26
  41.6 11.6 %fusion.190 = (f32[3,128,34,1]{3,1,2,0:T(8,128)}, f32[3,128,34,1]{3,1,2,0:T(8,128)}) fusion(f32[3,128,34,128]{3,1,2,0:T(8,128)} %pad_maximum_fusion), kind=kLoop, calls=%fused_computation.224 | loop fusion | bytes 208896 | tf_op jit(solution)/shard_map/slice | solution.py:24
  53.2 4.8 copy.69
  59.3 4.8 copy.71
  64.1 6.1 %collective-permute-start.3 = (f32[3,128,34,1]{1,2,3,0:T(8,128)S(1)}, f32[3,128,34,1]{1,2,3,0:T(8,128)S(1)}, u32[]{:S(2)}, u32[]{:S(2)}) collective-permute-start(f32[3,128,34,1]{1,2,3,0:T(8,128)S(1)} %copy.71), channel_id=1, source_target_pairs={{0,1},{1,2},{2,3},{3,4},{4,5},{5,6},{6,7},{8,9},{9,10},{10,11},{11... | collective-permute-start | bytes 156680 | tf_op jit(solution)/shard_map/ppermute | solution.py:28
  70.1 4.3 copy.70
  74.4 4.2 copy.72
  78.6 26.1 %multiply_convert_fusion.2 = bf16[3,128,32,128]{3,1,2,0:T(8,128)(2,1)S(1)} fusion(f32[3,128,32,128]{3,1,2,0:T(8,128)} %copy-done.1, f32[2,128,32,128]{3,1,2,0:T(8,128)} %slice_multiply_fusion, f32[3,128,1,128]{3,1,2,0:T(8,128)S(1)} %collective-permute-done, f32[3,128,1,128]{3,1,2,0:T(8,128)} %collective-permute-done.1, f32[3,128,34,1]{3,1,2,0:T(8,128)} %copy.72, ...), kind=kLoop, calls=%fused_computation.32 | loop fusion | flops 50331648 | bytes 33019904 | tf_op jit(solution)/shard_map/convert_element_type | solution.py:133
  107.4 25.5 %reshape.332 = bf16[8,3,8,16,2,16,16]{3,2,6,5,4,1,0:T(8,128)(2,1)} reshape(bf16[8,3,128,32,16]{2,4,3,1,0:T(8,128)(2,1)} %convert_bitcast_fusion) | data formatting | bytes 6291456 | tf_op jit(solution)/shard_map/reshape | solution.py:107
  132.9 35.8 %copy.73 = bf16[8,3,8,16,2,16,16]{6,5,3,1,0,4,2:T(8,128)(2,1)} copy(bf16[8,3,8,16,2,16,16]{3,2,6,5,4,1,0:T(8,128)(2,1)} %reshape.332) | data formatting | bytes 6291456 | tf_op jit(solution)/shard_map/reshape | solution.py:107
  168.7 46.1 %reshape.339 = bf16[128,12288]{1,0:T(8,128)(2,1)} reshape(bf16[8,2,8,3,16,16,16]{6,5,4,3,2,1,0:T(8,128)(2,1)} %bitcast.131) | data formatting | bytes 6291456 | tf_op jit(solution)/shard_map/reshape | solution.py:108
  214.8 8.4 %scatter_custom_fusion = bf16[128,12288]{1,0:T(8,128)(2,1)} fusion(s32[128]{0:T(128)S(1)} %fusion.175, bf16[128,12288]{1,0:T(8,128)(2,1)} %reshape.339, bf16[]{:T(256)} %constant.146.clone.1), kind=kCustom, calls=%fused_computation.83 | custom fusion | bytes 3146240 | tf_op jit(solution)/shard_map/scatter | solution.py:138
  223.6 5.6 %reduce = bf16[128,12288]{1,0:T(8,128)(2,1)} reduce(bf16[128,1,12288]{2,0,1:T(8,128)(2,1)} %bitcast.132, bf16[]{:T(256)} %broadcast.649), dimensions={1}, to_apply=%copy.74.reduce_sub_computation | reduce | bytes 6291458 | tf_op jit(solution)/shard_map/all_to_all | solution.py:139
  229.3 8.1 %reshape.349 = bf16[128,2,6144]{2,1,0:T(2,128)(2,1)} reshape(bf16[128,12288]{1,0:T(8,128)(2,1)} %reduce) | data formatting | bytes 6291456
  237.3 11.5 %all-to-all-start = ((bf16[128,2,6144]{2,1,0:T(2,128)(2,1)}), bf16[128,2,6144]{2,1,0:T(2,128)(2,1)}, u32[]{:S(2)}, u32[]{:S(2)}) async-start(bf16[128,2,6144]{2,1,0:T(2,128)(2,1)} %reshape.349), calls=%async_computation | async-start | bytes 6291456 | tf_op jit(solution)/shard_map/all_to_all | solution.py:139
  249.0 3.7 copy.84
  252.7 37.0 %all-to-all-done = bf16[128,2,6144]{2,1,0:T(2,128)(2,1)} async-done(((bf16[128,2,6144]{2,1,0:T(2,128)(2,1)}), bf16[128,2,6144]{2,1,0:T(2,128)(2,1)}, u32[]{:S(2)}, u32[]{:S(2)}) %all-to-all-start) | async-done | bytes 3145760 | tf_op jit(solution)/shard_map/all_to_all | solution.py:139
  289.7 19.4 %reshape.350 = bf16[128,1,12288]{2,1,0:T(2,128)(2,1)} reshape(bf16[128,2,6144]{2,1,0:T(2,128)(2,1)} %all-to-all-done) | data formatting | bytes 6291456
  309.0 13.1 %copy.75 = bf16[128,1,12288]{0,2,1:T(8,128)(2,1)S(1)} copy(bf16[128,1,12288]{2,1,0:T(2,128)(2,1)} %reshape.350) | data formatting | bytes 6291456 | tf_op jit(solution)/shard_map/all_to_all | solution.py:139
  329.2 3.5 fusion.91
  332.7 3.5 fusion.96
  336.3 3.7 fusion.101
  349.3 4.6 multiply_convert_fusion.1
  355.9 6.0 %multiply_convert_fusion = (bf16[256,8192]{0,1:T(8,128)(2,1)}, f32[256,8192]{0,1:T(8,128)}) fusion(f32[256]{0:T(256)S(1)} %copy-done.14, bf16[256,8192]{0,1:T(8,128)(2,1)S(1)} %get-tuple-element.49, bf16[256,256]{1,0:T(8,128)(2,1)S(1)} %copy-done), kind=kOutput, calls=%fused_computation.15 | convolution fusion | flops 1086324736 | bytes 16909312 | tf_op jit(solution)/shard_map/dot_general | solution.py:147
  362.2 4.7 convert_reduce_fusion.2
  366.9 5.9 %convert_reduce_fusion = (f32[256]{0:T(256)S(1)}, bf16[256,8192]{0,1:T(8,128)(2,1)S(1)}) fusion(f32[256,8192]{0,1:T(8,128)} %get-tuple-element.52, bf16[6,8192]{1,0:T(8,128)(2,1)S(1)} %get-tuple-element.34, bf16[6,256]{1,0:T(8,128)(2,1)S(1)} %copy-done.9), kind=kOutput, calls=%fused_computation.13 | convolution fusion | flops 48234240 | bytes 12685312 | tf_op jit(solution)/shard_map/dot_general | solution.py:158
  376.8 7.7 %convert_reduce_fusion.1 = (f32[256]{0:T(256)S(1)}, bf16[256,8192]{0,1:T(8,128)(2,1)S(1)}) fusion(f32[256,8192]{0,1:T(8,128)} %get-tuple-element.50, bf16[256,8192]{0,1:T(8,128)(2,1)} %copy-done.5, bf16[256,256]{1,0:T(8,128)(2,1)S(1)} %copy-done), kind=kOutput, calls=%fused_computation.14 | convolution fusion | flops 1096810240 | bytes 16909312 | tf_op jit(solution)/shard_map/dot_general | solution.py:166
  385.8 64.0 %all-reduce.1 = (f32[]{:T(128)}, f32[256,24]{0,1:T(8,128)}, f32[256]{0:T(256)}, f32[256]{0:T(256)}, f32[6,256]{1,0:T(8,128)}, /*index=5*/f32[6]{0:T(128)}) all-reduce(f32[]{:T(128)} %get-tuple-element.48, f32[256,24]{0,1:T(8,128)S(1)} %fusion.197, f32[256]{0:T(256)S(1)} %get-tuple-element.54, ...), channel_id=1, replica_groups=mesh['gy'=16,'gz'=8] {'gy','gz'}, use_global_device_ids=true, to_apply=%region_3.4 | all-reduce | flops 8199 | bytes 65592 | tf_op jit(solution)/shard_map/psum | solution.py:173
  450.5 64.9 %all-reduce.4.cloned.1.call-done = f32[256,256]{1,0:T(8,128)} async-done(((f32[256,256]{1,0:T(8,128)}), f32[256,256]{1,0:T(8,128)}) %all-reduce.4.cloned.1.call-update) | async-done | bytes 262160 | tf_op jit(solution)/shard_map/psum | solution.py:173
  (78 shorter events, 41.8 us)
Async XLA Ops:
  7.2 348.7 %copy-start = (bf16[256,256]{1,0:T(8,128)(2,1)S(1)}, bf16[256,256]{1,0:T(8,128)(2,1)}, u32[]{:S(2)}) copy-start(bf16[256,256]{1,0:T(8,128)(2,1)} %param.16) | copy-start | bytes 393220
  14.4 18.2 %copy-start.1 = (f32[3,128,32,128]{3,1,2,0:T(8,128)}, f32[3,128,32,128]{3,1,2,0:T(8,128)S(1)}, u32[]{:S(2)}) copy-start(f32[3,128,32,128]{3,1,2,0:T(8,128)S(1)} %copy_multiply_fusion) | copy-start | bytes 18874372
  15.2 19.9 %collective-permute-start = (f32[3,128,1,128]{3,1,2,0:T(8,128)}, f32[3,128,1,128]{3,1,2,0:T(8,128)S(1)}, u32[]{:S(2)}, u32[]{:S(2)}) collective-permute-start(f32[3,128,1,128]{3,1,2,0:T(8,128)} %get-tuple-element.45), channel_id=1, source_target_pairs={{8,0},{16,8},{24,16},{32,24},{40,32},{48,40},{56,48},{64,56},{72,6... | collective-permute-start | bytes 589832 | tf_op jit(solution)/shard_map/ppermute | solution.py:30
  18.6 16.6 %collective-permute-start.1 = (f32[3,128,1,128]{3,1,2,0:T(8,128)}, f32[3,128,1,128]{3,1,2,0:T(8,128)}, u32[]{:S(2)}, u32[]{:S(2)}) collective-permute-start(f32[3,128,1,128]{3,1,2,0:T(8,128)} %get-tuple-element.44), channel_id=1, source_target_pairs={{0,8},{8,16},{16,24},{24,32},{32,40},{40,48},{48,56},{56,64},{64,7... | collective-permute-start | bytes 589832 | tf_op jit(solution)/shard_map/ppermute | solution.py:28
  25.0 7.5 %copy-start.7 = (s32[32,128]{1,0:T(8,128)S(1)}, s32[32,128]{1,0:T(8,128)}, u32[]{:S(2)}) copy-start(s32[32,128]{1,0:T(8,128)} %param.12) | copy-start | bytes 49156
  31.3 3.7 copy-start.8
  32.6 2.5 copy-start.11
  58.0 12.2 %collective-permute-start.2 = (f32[3,128,34,1]{1,2,3,0:T(8,128)S(1)}, f32[3,128,34,1]{1,2,3,0:T(8,128)S(1)}, u32[]{:S(2)}, u32[]{:S(2)}) collective-permute-start(f32[3,128,34,1]{1,2,3,0:T(8,128)S(1)} %copy.69), channel_id=1, source_target_pairs={{1,0},{2,1},{3,2},{4,3},{5,4},{6,5},{7,6},{9,8},{10,9},{11,10},{12... | collective-permute-start | bytes 156680 | tf_op jit(solution)/shard_map/ppermute | solution.py:30
  64.1 10.4 %collective-permute-start.3 = (f32[3,128,34,1]{1,2,3,0:T(8,128)S(1)}, f32[3,128,34,1]{1,2,3,0:T(8,128)S(1)}, u32[]{:S(2)}, u32[]{:S(2)}) collective-permute-start(f32[3,128,34,1]{1,2,3,0:T(8,128)S(1)} %copy.71), channel_id=1, source_target_pairs={{0,1},{1,2},{2,3},{3,4},{4,5},{5,6},{6,7},{8,9},{9,10},{10,11},{11... | collective-permute-start | bytes 156680 | tf_op jit(solution)/shard_map/ppermute | solution.py:28
  237.3 52.4 %all-to-all-start = ((bf16[128,2,6144]{2,1,0:T(2,128)(2,1)}), bf16[128,2,6144]{2,1,0:T(2,128)(2,1)}, u32[]{:S(2)}, u32[]{:S(2)}) async-start(bf16[128,2,6144]{2,1,0:T(2,128)(2,1)} %reshape.349), calls=%async_computation | async-start | bytes 6291456 | tf_op jit(solution)/shard_map/all_to_all | solution.py:139
  248.8 266.6 %all-reduce.4.cloned.1.call-start = ((), (), s32[]{:S(2)}) async-start(), calls=%async_computation.1 | async-start | bytes 524288 | tf_op jit(solution)/shard_map/psum | solution.py:173
  332.7 14.2 %copy-start.6 = (bf16[3,8,128,64]{2,3,1,0:T(8,128)(2,1)S(1)}, bf16[3,8,128,64]{2,3,1,0:T(8,128)(2,1)}, u32[]{:S(2)}) copy-start(bf16[3,8,128,64]{2,3,1,0:T(8,128)(2,1)} %get-tuple-element.47) | copy-start | bytes 1179652
  336.2 13.1 %copy-start.12 = (bf16[256,24]{0,1:T(8,128)(2,1)S(1)}, bf16[256,24]{0,1:T(8,128)(2,1)}, u32[]{:S(2)}) copy-start(bf16[256,24]{0,1:T(8,128)(2,1)} %param.14) | copy-start | bytes 36868
  336.3 13.1 %copy-start.13 = (f32[256]{0:T(256)S(1)}, f32[256]{0:T(256)}, u32[]{:S(2)}) copy-start(f32[256]{0:T(256)} %param.15) | copy-start | bytes 3076
  349.3 6.6 %copy-start.14 = (f32[256]{0:T(256)S(1)}, f32[256]{0:T(256)}, u32[]{:S(2)}) copy-start(f32[256]{0:T(256)} %param.17) | copy-start | bytes 3076
  353.9 2.0 copy-start.3
  355.9 6.3 %copy-start.9 = (bf16[6,256]{1,0:T(8,128)(2,1)S(1)}, bf16[6,256]{1,0:T(8,128)(2,1)}, u32[]{:S(2)}) copy-start(bf16[6,256]{1,0:T(8,128)(2,1)} %param.18) | copy-start | bytes 9220
  355.9 6.3 %copy-start.10 = (f32[6]{0:T(128)S(1)}, f32[6]{0:T(128)}, u32[]{:S(2)}) copy-start(f32[6]{0:T(128)} %param.19) | copy-start | bytes 76
  366.9 7.8 %copy-start.4 = (bf16[256,8192]{0,1:T(8,128)(2,1)S(1)}, bf16[256,8192]{0,1:T(8,128)(2,1)}, u32[]{:S(2)}) copy-start(bf16[256,8192]{0,1:T(8,128)(2,1)} %copy-done.3) | copy-start | bytes 12582916
  372.8 2.0 copy-start.5
  376.8 8.4 %copy-start.2 = (bf16[256,8192]{0,1:T(8,128)(2,1)S(1)}, bf16[256,8192]{0,1:T(8,128)(2,1)}, u32[]{:S(2)}) copy-start(bf16[256,8192]{0,1:T(8,128)(2,1)} %get-tuple-element.51) | copy-start | bytes 12582916
Sparse Core Ops, SparseCore 0:
  376.9 138.4 all-reduce.3
where the time goes:
time: 536 us; the launch traced here: 525 us
  local copies, waits for them, and re-layouts  206 us (38%)
  waiting for transfers between devices  102 us (19%)
  blocking collectives  64 us (12%)
  matrix products  59.1 us (11%)
  other arithmetic  51.8 us (10%)
  starting transfers between devices  25.7 us (5%)
  between operations  16.7 us (3%)
    psum x1, waiting for transfers between devices, on_device(): lax.psum((grad_w_in, grad_b_in, grad_w_mid, grad_b_mid, grad_w_out, grad_...  64.9 us
    psum x1, blocking collectives, on_device(): lax.psum((grad_w_in, grad_b_in, grad_w_mid, grad_b_mid, grad_w_out, grad_...  64 us
    reshape x2, local copies, waits for them, and re-layouts, cut_tiles(): moved.reshape(groups, 3, STATIONS // TILE, TILE, width // TILE, TILE, TILE)  61.3 us
    reshape x1, local copies, waits for them, and re-layouts, cut_tiles(): return moved.transpose(2, 4, 0, 1, 3, 5, 6).reshape(-1, 3 * TILE ** 3)  46.1 us
    all_to_all x1, waiting for transfers between devices, on_device(): lax.all_to_all(ordered, ('gy', 'gz'), split_axis=0, concat_axis=0, tiled=...  37 us
    unnamed x34, local copies, waits for them, and re-layouts  36.8 us
    convert_element_type x1, other arithmetic, on_device(): ((masked + time_step * (viscosity * laplace - advect + lorentz)) * fluid)...  26.1 us
    dot_general x6, matrix products, assemble(): jnp.dot(values[:, left_comp] * values[:, right_comp], point_pool, precisi...  21.1 us
  transfers between devices with their start and end apart: 6, of which 2 were waited for; matrix products, arithmetic and copies ran while one was open for 7% of the time, Pallas kernels for 0%

commit v1 on v0

v1 whole, which is shorter than its diff:
```python
import functools

import jax
import jax.numpy as jnp
from jax import lax
from jax.experimental import pallas as pl
from jax.experimental.pallas import tpu as pltpu
from jax.sharding import PartitionSpec as P

MESH = pl.DeviceIdType.MESH
STATIONS = 128
CY = 32
CZ = 128
HID = 256
N_GY = 16
N_GZ = 8
TILES = 128
SAMPLES = 1048576
ROWS = 3 * STATIONS * CY
SLABS = 8
LANES = 1024
PART = 512
F32 = jnp.float32
BF16 = jnp.bfloat16
PAIRS = ((0, 0), (1, 1), (2, 2), (0, 1), (0, 2), (1, 2))
NT = (((1,), (1,)), ((), ()))


def iota(shape, dim):
    return lax.broadcasted_iota(jnp.int32, shape, dim)


def wait_bytes(ref, sem):
    pltpu.make_async_copy(ref, ref, sem).wait()


def pack_edges(v, fluid, edge_lo, edge_hi, columns):
    for c in range(3):
        first = c * STATIONS * CY
        edge_lo[pl.ds(c * STATIONS, STATIONS), :] = v[pl.ds(first, STATIONS, stride=CY), :] * fluid[0:1, :]
        edge_hi[pl.ds(c * STATIONS, STATIONS), :] = (
            v[pl.ds(first + CY - 1, STATIONS, stride=CY), :] * fluid[CY - 1 : CY, :]
        )
    pair = iota((8, 128), 1) // 2

    def station(s, acc):
        here = pair == s
        out = []
        for c in range(3):
            for h in range(2):
                for j in range(4):
                    cells = v[pl.ds((c * STATIONS + h * 64 + s) * CY + 8 * j, 8), :]
                    moved = pltpu.roll(cells, 2 * s + 1, 1)
                    out.append(jnp.where(here, moved, acc[len(out)]))
        return tuple(out)

    packed = lax.fori_loop(0, 64, station, tuple(jnp.zeros((8, 128), F32) for _ in range(24)))
    odd = iota((8, 128), 1) % 2 == 1
    for c in range(3):
        for h in range(2):
            for j in range(4):
                mask = fluid[8 * j : 8 * j + 8, :]
                ends = jnp.where(odd, mask[:, 0:1], mask[:, CZ - 1 : CZ])
                columns[pl.ds((c * 2 + h) * CY + 8 * j, 8), :] = packed[(c * 2 + h) * 4 + j] * ends


def halo_kernel(vel, wall, lo_out, hi_out, col_out, v, fluid, edge_lo, edge_hi, columns, got_lo, got_hi, got_left, got_right, load, send, recv):
    y = lax.axis_index("gy")
    z = lax.axis_index("gz")
    below = ((y + N_GY - 1) % N_GY, z)
    above = ((y + 1) % N_GY, z)
    left = (y, (z + N_GZ - 1) % N_GZ)
    right = (y, (z + 1) % N_GZ)
    fetch = pltpu.make_async_copy(vel, v, load)
    fetch.start()
    barrier = pltpu.get_barrier_semaphore()
    for peer in (below, above, left, right):
        pl.semaphore_signal(barrier, inc=1, device_id=peer, device_id_type=MESH)
    fluid[...] = (1 - wall[...]).astype(F32)
    fetch.wait()
    pack_edges(v, fluid, edge_lo, edge_hi, columns)
    pl.semaphore_wait(barrier, 4)
    copies = []
    for k, (src, dst, peer) in enumerate(
        ((edge_lo, got_hi, below), (edge_hi, got_lo, above), (columns, got_right, left), (columns, got_left, right))
    ):
        copy = pltpu.make_async_remote_copy(
            src, dst, send.at[k], recv.at[k], device_id=peer, device_id_type=MESH
        )
        copy.start()
        copies.append(copy)
    for copy in copies:
        copy.wait()
    lo_out[...] = got_lo[...] * jnp.where(y > 0, 1.0, 0.0)
    hi_out[...] = got_hi[...] * jnp.where(y < N_GY - 1, 1.0, 0.0)
    has_left = jnp.where(z > 0, 1.0, 0.0)
    has_right = jnp.where(z < N_GZ - 1, 1.0, 0.0)
    odd = iota((8, 128), 1) % 2 == 1
    for k in range(24):
        rows = pl.ds(8 * k, 8)
        col_out[rows, :] = jnp.where(odd, got_right[rows, :] * has_right, pltpu.roll(got_left[rows, :] * has_left, 2, 1))


def halo_call(vel, wall):
    return pl.pallas_call(
        halo_kernel,
        name="halo",
        out_shape=[
            jax.ShapeDtypeStruct((384, 128), F32),
            jax.ShapeDtypeStruct((384, 128), F32),
            jax.ShapeDtypeStruct((192, 128), F32),
        ],
        in_specs=[pl.BlockSpec(memory_space=pl.ANY), pl.BlockSpec(memory_space=pltpu.VMEM)],
        out_specs=[pl.BlockSpec(memory_space=pltpu.VMEM)] * 3,
        scratch_shapes=[
            pltpu.VMEM((ROWS, 128), F32),
            pltpu.VMEM((CY, 128), F32),
            pltpu.VMEM((384, 128), F32),
            pltpu.VMEM((384, 128), F32),
            pltpu.VMEM((192, 128), F32),
            pltpu.VMEM((384, 128), F32),
            pltpu.VMEM((384, 128), F32),
            pltpu.VMEM((192, 128), F32),
            pltpu.VMEM((192, 128), F32),
            pltpu.SemaphoreType.DMA,
            pltpu.SemaphoreType.DMA((4,)),
            pltpu.SemaphoreType.DMA((4,)),
        ],
        compiler_params=pltpu.CompilerParams(collective_id=0, has_side_effects=True, vmem_limit_bytes=24 << 20),
    )(vel, wall)


def stencil_station(v, lo, hi, col, tables, stepped, rounded, st, s):
    ahead = lax.rem(st + 1, STATIONS)
    behind = lax.rem(st + STATIONS - 1, STATIONS)
    half = st // 64
    shift = 126 - 2 * lax.rem(st, 64)
    first_row = iota((8, 128), 0) == 0
    last_row = iota((8, 128), 0) == 7
    first_lane = iota((8, 128), 1) == 0
    last_lane = iota((8, 128), 1) == CZ - 1

    def cells(c, t, j):
        return v[pl.ds((c * STATIONS + t) * CY + 8 * j, 8), :]

    m = [[cells(c, st, j) * tables[pl.ds(8 * j, 8), :] for j in range(4)] for c in range(3)]
    minus = [[1.0 - m[c][j] for j in range(4)] for c in range(3)]
    plus = [[1.0 + m[c][j] for j in range(4)] for c in range(3)]
    for c in range(3):
        edge_lo = jnp.broadcast_to(lo[pl.ds(c * STATIONS + st, 1), :], (8, 128))
        edge_hi = jnp.broadcast_to(hi[pl.ds(c * STATIONS + st, 1), :], (8, 128))
        down = [edge_lo] + [pltpu.roll(m[c][j], 1, 0) for j in range(4)]
        up = [pltpu.roll(m[c][j], 7, 0) for j in range(4)] + [edge_hi]
        results = []
        for j in range(4):
            south = jnp.where(first_row, down[j], down[j + 1])
            north = jnp.where(last_row, up[j + 1], up[j])
            ends = pltpu.roll(col[pl.ds((c * 2 + half) * CY + 8 * j, 8), :], shift, 1)
            lower = jnp.where(first_lane, ends, pltpu.roll(m[c][j], 1, 1))
            upper = jnp.where(last_lane, ends, pltpu.roll(m[c][j], CZ - 1, 1))
            total = minus[0][j] * cells(c, ahead, j) + plus[0][j] * cells(c, behind, j)
            total = total + (minus[1][j] * north + plus[1][j] * south)
            total = total + (minus[2][j] * upper + plus[2][j] * lower)
            own = tables[pl.ds(64 + 8 * j, 8), :] if c < 2 else 4.0
            total = total + own * m[c][j]
            results.append(total * tables[pl.ds(32 + 8 * j, 8), :])
        for k in range(2):
            value = jnp.concatenate(results[2 * k : 2 * k + 2], axis=0).astype(BF16)
            stepped[pl.ds(pl.multiple_of((c * STATIONS + st) * CY + 16 * k, 16), 16), :] = value
            rounded[pl.ds((c * 16 + s) * CY + 16 * k, 16), :] = value.astype(F32)


def pool_slab(rounded, feat):
    residue = iota((8, 128), 1) % 4
    merged = [None] * 30

    def put(f, r, value, source):
        shift = (r - source) % 128
        value = pltpu.roll(value, shift, 1) if shift else value
        merged[f] = value if merged[f] is None else jnp.where(residue == r, value, merged[f])

    for r in range(4):
        sums = [[None] * 4 for _ in range(3)]
        products = [None] * 6
        for dx in range(4):
            for dy in range(4):
                q = (dx // 2) * 2 + dy // 2
                u = [rounded[pl.ds((c * 16 + 4 * r + dx) * CY + dy, 8, stride=4), :] for c in range(3)]
                for c in range(3):
                    sums[c][q] = u[c] if sums[c][q] is None else sums[c][q] + u[c]
                for k, (a, b) in enumerate(PAIRS):
                    value = u[a] * u[b]
                    products[k] = value if products[k] is None else products[k] + value
        means = []
        for c in range(3):
            point = None
            for q in range(4):
                two = sums[c][q] + pltpu.roll(sums[c][q], 127, 1)
                put(c * 8 + 2 * q, r, two, 0)
                put(c * 8 + 2 * q + 1, r, two, 2)
                point = two if point is None else point + two
            means.append((point + pltpu.roll(point, 126, 1)) * (1.0 / 64))
        for k, (a, b) in enumerate(PAIRS):
            two = products[k] + pltpu.roll(products[k], 127, 1)
            four = two + pltpu.roll(two, 126, 1)
            put(24 + k, r, four * (1.0 / 64) - means[a] * means[b], 0)
    for f in range(24):
        feat[pl.ds(8 * f, 8), :] = merged[f] * 0.125
    for f in range(24, 30):
        feat[pl.ds(8 * f, 8), :] = merged[f].astype(BF16).astype(F32)


def column_table(row):
    wide = jnp.broadcast_to(row, (128, HID))
    return jnp.concatenate([jnp.transpose(wide[:, :128]), jnp.transpose(wide[:, 128:])], axis=0)


def prepare_weights(w_in, b_in, w_mid, b_mid, w_out, b_out, win, wmid, wmid_t, wout, wout_t, bias_mid, bias_out, tmp):
    lane = iota((HID, 128), 1)
    bias = column_table(b_in[...]) * 0.5
    high = bias.astype(BF16).astype(F32)
    tmp[...] = jnp.zeros_like(tmp)
    tmp[:, 0:24] = w_in[...].astype(F32) * 0.5
    full = tmp[...]
    full = jnp.where(lane == 30, high, jnp.where(lane == 31, bias - high, full))
    win[...] = full[:, 0:32].astype(BF16)
    mid = w_mid[...].astype(F32) * 0.5
    wmid[...] = mid.astype(BF16)
    wmid_t[...] = jnp.transpose(mid).astype(BF16)
    bias_mid[...] = column_table(b_mid[...]) * 0.5
    for h in range(2):
        tmp[pl.ds(0, 128), :] = jnp.zeros((128, 128), F32)
        tmp[pl.ds(0, 6), :] = w_out[:, 128 * h : 128 * h + 128].astype(F32)
        wout[:, 128 * h : 128 * h + 128] = tmp[pl.ds(0, 16), :].astype(BF16)
        wout_t[pl.ds(128 * h, 128), :] = (jnp.transpose(tmp[pl.ds(0, 128), :])[:, 0:16] * 0.5).astype(BF16)
    row = iota((8, 128), 0)
    table = jnp.where(row >= 6, 1.0, 0.0)
    for k in range(6):
        table = jnp.where(row == k, b_out[k], table)
    bias_out[...] = table


def widen(table, lanes):
    return jnp.concatenate([table] * (lanes // 128), axis=1)


def lane_sum(value):
    total = value[:, 0:128]
    for k in range(1, value.shape[1] // 128):
        total = total + value[:, 128 * k : 128 * k + 128]
    return total


def train_part(x, targets, win, wmid, wmid_t, wout, wout_t, bias_mid, bias_out, pred, g_in, g_mid, g_out, g_bmid, g_bout, g_loss):
    n = x.shape[1]
    h1 = jnp.dot(win[...], x, preferred_element_type=F32)
    t1 = jnp.tanh(h1)
    p1 = 1.0 + t1
    a1 = h1 * p1
    slope1 = p1 + a1 * (2.0 - p1)
    act1 = a1.astype(BF16)
    h2 = jnp.dot(wmid[...], act1, preferred_element_type=F32) + widen(bias_mid[...], n)
    p2 = 1.0 + jnp.tanh(h2)
    a2 = h2 * p2
    slope2 = p2 + a2 * (2.0 - p2)
    act2 = a2.astype(BF16)
    prediction = jnp.dot(wout[...], act2, preferred_element_type=F32)[0:8] + widen(bias_out[...], n)
    pred[...] = prediction
    residual = prediction - targets
    g_loss[...] += lane_sum(residual * residual)
    grad = (residual * (2.0 / (6 * SAMPLES))).astype(BF16).astype(F32)
    g_bout[...] += lane_sum(grad)
    grad = jnp.concatenate([grad, jnp.zeros_like(grad)], axis=0).astype(BF16)
    g_out[...] += lax.dot_general(grad, act2, NT, preferred_element_type=F32)
    d2 = jnp.dot(wout_t[...], grad, preferred_element_type=F32) * slope2
    g_bmid[...] += lane_sum(d2)
    grad2 = d2.astype(BF16)
    g_mid[...] += lax.dot_general(grad2, act1, NT, preferred_element_type=F32)
    d1 = jnp.dot(wmid_t[...], grad2, preferred_element_type=F32) * slope1
    grad1 = d1.astype(BF16)
    g_in[...] += lax.dot_general(x, grad1, NT, preferred_element_type=F32)


def scatter_slab(a, pred, table, ordered):
    lane = iota((8, 128), 1)
    point = lane % 64
    quarter = point // 4 % 4
    source = 4 * (point % 4) + point // 16
    low = lane < 64
    for b in range(2):
        blocks = [pred[:, 128 * (4 * b + q) : 128 * (4 * b + q) + 128] for q in range(4)]
        for c in range(8):
            index = source + 16 * c
            value = jnp.take_along_axis(blocks[0], index, axis=1)
            for q in range(1, 4):
                value = jnp.where(quarter == q, jnp.take_along_axis(blocks[q], index, axis=1), value)
            value = jnp.where(low, value, pltpu.roll(value, 5, 0))
            ordered[table[a * 16 + b * 8 + c]] = value[0:3]


def main_kernel(
    vel, wall, hart, table, lo, hi, col, w_in, b_in, w_mid, b_mid, w_out, b_out,
    stepped_out, grads, ordered,
    v, stepped, rounded, tables, feat, xs, targets, pred, win, wmid, wmid_t, wout, wout_t, bias_mid, bias_out, tmp,
    g_in, g_mid, g_out, g_bmid, g_bout, g_loss, load, store,
):
    def fetch(c, i):
        rows = pl.ds(c * STATIONS * CY + i * 16 * CY, 16 * CY)
        return pltpu.make_async_copy(vel.at[rows], v.at[rows], load.at[i])

    def fetches(i, act):
        for c in range(3):
            getattr(fetch(c, i), act)()

    def store_copy(c, a):
        rows = pl.ds(pl.multiple_of(c * STATIONS * CY + a * 16 * CY, 16), 16 * CY)
        return pltpu.make_async_copy(stepped.at[rows], stepped_out.at[rows], store.at[c])

    for i in (7, 0, 1, 2, 3, 4, 5, 6):
        fetches(i, "start")
    fluid = (1 - wall[...]).astype(F32)
    tables[pl.ds(0, 32), :] = fluid
    tables[pl.ds(32, 32), :] = fluid * 0.1
    tables[pl.ds(64, 32), :] = 2.0 - 2.0 * hart[...].astype(F32)
    prepare_weights(w_in, b_in, w_mid, b_mid, w_out, b_out, win, wmid, wmid_t, wout, wout_t, bias_mid, bias_out, tmp)
    for ref in (g_in, g_mid, g_out, g_bmid, g_bout, g_loss):
        ref[...] = jnp.zeros_like(ref)
    feat[pl.ds(240, 16), :] = jnp.ones((16, 128), F32)
    for i in (7, 0, 1, 2, 3, 4, 5, 6):
        fetches(i, "wait")

    def slab(a, carry):
        def station(s, inner):
            stencil_station(v, lo, hi, col, tables, stepped, rounded, a * 16 + s, s)
            return inner

        lax.fori_loop(0, 16, station, 0)
        for c in range(3):
            store_copy(c, a).start()
        pool_slab(rounded, feat)
        for yp in range(8):
            lanes = slice(128 * yp, 128 * yp + 128)
            xs[:, lanes] = feat[pl.ds(yp, 32, stride=8), :].astype(BF16)
            targets[:, lanes] = feat[pl.ds(192 + yp, 8, stride=8), :]
        for k in range(LANES // PART):
            lanes = slice(PART * k, PART * k + PART)
            train_part(
                xs[:, lanes], targets[:, lanes], win, wmid, wmid_t, wout, wout_t, bias_mid, bias_out,
                pred.at[:, lanes], g_in, g_mid, g_out, g_bmid, g_bout, g_loss,
            )
        scatter_slab(a, pred, table, ordered)
        return carry

    lax.fori_loop(0, SLABS, slab, 0)
    for c in range(3):
        wait_bytes(stepped.at[pl.ds(0, STATIONS * CY)], store.at[c])
    for t in range(64):
        grads[t // 5, t % 5] = g_mid[pl.ds(8 * (t // 2), 8), 128 * (t % 2) : 128 * (t % 2) + 128]
    for k in range(8):
        t = 64 + k
        grads[t // 5, t % 5] = g_in[pl.ds(8 * (k // 2), 8), 128 * (k % 2) : 128 * (k % 2) + 128]
    row = iota((8, 128), 0)
    lane = iota((8, 128), 1)
    sums_out = jnp.sum(g_bout[...], axis=1, keepdims=True)
    last = jnp.sum(jnp.where((lane == row + 8) & (row < 6), sums_out, 0.0), axis=0, keepdims=True)
    loss = jnp.sum(jnp.sum(g_loss[...], axis=1, keepdims=True), axis=0, keepdims=True)
    last = jnp.where(lane[0:1] == 0, loss, last)
    for k in range(2):
        t = 72 + k
        bias = jnp.sum(jnp.transpose(g_bmid[pl.ds(128 * k, 128), :]), axis=0, keepdims=True)
        value = g_out[pl.ds(0, 8), 128 * k : 128 * k + 128]
        grads[t // 5, t % 5] = jnp.where(row == 6, bias, jnp.where(row == 7, last, value))
    for t in range(74, 80):
        grads[t // 5, t % 5] = jnp.zeros((8, 128), F32)


def main_call(vel, wall, hart, table, lo, hi, col, w_in, b_in, w_mid, b_mid, w_out, b_out):
    vm = pl.BlockSpec(memory_space=pltpu.VMEM)
    sm = pl.BlockSpec(memory_space=pltpu.SMEM)
    anywhere = pl.BlockSpec(memory_space=pl.ANY)
    return pl.pallas_call(
        main_kernel,
        name="step_train",
        out_shape=[
            jax.ShapeDtypeStruct((ROWS, 128), BF16),
            jax.ShapeDtypeStruct((16, 5, 8, 128), F32),
            jax.ShapeDtypeStruct((TILES, 3, 128), F32),
        ],
        in_specs=[anywhere, vm, vm, sm, vm, vm, vm, vm, vm, vm, vm, vm, sm],
        out_specs=[anywhere, vm, vm],
        scratch_shapes=[
            pltpu.VMEM((ROWS, 128), F32),
            pltpu.VMEM((ROWS, 128), BF16),
            pltpu.VMEM((3 * 16 * CY, 128), F32),
            pltpu.VMEM((96, 128), F32),
            pltpu.VMEM((256, 128), F32),
            pltpu.VMEM((32, LANES), BF16),
            pltpu.VMEM((8, LANES), F32),
            pltpu.VMEM((8, LANES), F32),
            pltpu.VMEM((HID, 32), BF16),
            pltpu.VMEM((HID, HID), BF16),
            pltpu.VMEM((HID, HID), BF16),
            pltpu.VMEM((16, HID), BF16),
            pltpu.VMEM((HID, 16), BF16),
            pltpu.VMEM((HID, 128), F32),
            pltpu.VMEM((8, 128), F32),
            pltpu.VMEM((HID, 128), F32),
            pltpu.VMEM((32, HID), F32),
            pltpu.VMEM((HID, HID), F32),
            pltpu.VMEM((16, HID), F32),
            pltpu.VMEM((HID, 128), F32),
            pltpu.VMEM((8, 128), F32),
            pltpu.VMEM((8, 128), F32),
            pltpu.SemaphoreType.DMA((8,)),
            pltpu.SemaphoreType.DMA((3,)),
        ],
        compiler_params=pltpu.CompilerParams(vmem_limit_bytes=48 << 20),
    )(vel, wall, hart, table, lo, hi, col, w_in, b_in, w_mid, b_mid, w_out, b_out)


def share_kernel(
    g, p, pred_out, loss_out, in_out, bin_out, mid_out, bmid_out, out_out, bout_out,
    part, mine, column, total, hop, got, s0, r0, s1, r1, s2, r2, s3, r3, s4, r4,
):
    y = lax.axis_index("gy")
    z = lax.axis_index("gz")
    barrier = pltpu.get_barrier_semaphore()
    for d in range(1, N_GY):
        pl.semaphore_signal(barrier, inc=1, device_id=((y + d) % N_GY, z), device_id_type=MESH)
    for d in range(1, N_GZ):
        pl.semaphore_signal(barrier, inc=1, device_id=(y, (z + d) % N_GZ), device_id_type=MESH)
    pl.semaphore_wait(barrier, N_GY + N_GZ - 2)

    def send(src, dst, ss, rs, qy, qz):
        pltpu.make_async_remote_copy(src, dst, ss, rs, device_id=(qy, qz), device_id_type=MESH).start()

    for d in range(1, N_GY):
        q = (y + d) % N_GY
        send(g.at[q], part.at[y], s0, r0, q, z)
    for d in range(1, N_GZ):
        q = (z + d) % N_GZ
        send(p.at[:, q], hop.at[z], s1, r1, y, q)
    hop[z] = p[:, z]
    part[y] = g[y]
    wait_bytes(part.at[pl.ds(0, N_GY - 1)], r0)
    column[z] = jnp.sum(part[...], axis=0)
    for d in range(1, N_GZ):
        q = (z + d) % N_GZ
        send(column.at[z], column.at[z], s2, r2, y, q)
    wait_bytes(hop.at[pl.ds(0, N_GZ - 1)], r1)
    for d in range(1, N_GY):
        q = (y + d) % N_GY
        send(hop.at[:, q], got.at[y], s3, r3, q, z)
    got[y] = hop[:, y]
    wait_bytes(column.at[pl.ds(0, N_GZ - 1)], r2)
    mine[...] = jnp.sum(column[...], axis=0)
    for d in range(1, N_GY):
        q = (y + d) % N_GY
        send(mine, total.at[y], s4, r4, q, z)
    total[y] = mine[...]
    wait_bytes(got.at[pl.ds(0, N_GY - 1)], r3)
    low = iota((3, 128), 1) < 64
    for j in range(TILES // 2):
        first = got[(2 * j) // N_GZ, (2 * j) % N_GZ]
        second = got[(2 * j + 1) // N_GZ, (2 * j + 1) % N_GZ]
        lanes = slice(128 * j, 128 * j + 128)
        pred_out[0:3, lanes] = jnp.where(low, first, pltpu.roll(second, 64, 1))
        pred_out[3:6, lanes] = jnp.where(low, pltpu.roll(first, 64, 1), second)
    wait_bytes(total.at[pl.ds(0, N_GY - 1)], r4)
    for t in range(64):
        mid_out[pl.ds(8 * (t // 2), 8), 128 * (t % 2) : 128 * (t % 2) + 128] = total[t // 5, t % 5]
    for h in range(2):
        rows = jnp.concatenate([total[(64 + 2 * k + h) // 5, (64 + 2 * k + h) % 5] for k in range(4)], axis=0)
        padded = jnp.concatenate([rows, jnp.zeros((96, 128), F32)], axis=0)
        in_out[pl.ds(128 * h, 128), :] = jnp.transpose(padded)[:, 0:24]
        bin_out[:, 128 * h : 128 * h + 128] = rows[30:31]
        last = total[(72 + h) // 5, (72 + h) % 5]
        out_out[:, 128 * h : 128 * h + 128] = last[0:6]
        bmid_out[:, 128 * h : 128 * h + 128] = last[6:7]
        if h == 0:
            loss_out[...] = last[7:8] * (1.0 / (6 * SAMPLES))
            bout_out[...] = last[7:8]
    wait_bytes(part.at[pl.ds(0, N_GY - 1)], s0)
    wait_bytes(hop.at[pl.ds(0, N_GZ - 1)], s1)
    wait_bytes(column.at[pl.ds(0, N_GZ - 1)], s2)
    wait_bytes(got.at[pl.ds(0, N_GY - 1)], s3)
    wait_bytes(total.at[pl.ds(0, N_GY - 1)], s4)


def share_call(grads, ordered):
    vm = pl.BlockSpec(memory_space=pltpu.VMEM)
    return pl.pallas_call(
        share_kernel,
        name="share",
        out_shape=[
            jax.ShapeDtypeStruct((6, 64 * 128), F32),
            jax.ShapeDtypeStruct((1, 128), F32),
            jax.ShapeDtypeStruct((HID, 24), F32),
            jax.ShapeDtypeStruct((1, HID), F32),
            jax.ShapeDtypeStruct((HID, HID), F32),
            jax.ShapeDtypeStruct((1, HID), F32),
            jax.ShapeDtypeStruct((6, HID), F32),
            jax.ShapeDtypeStruct((1, 128), F32),
        ],
        in_specs=[vm, vm],
        out_specs=[vm] * 8,
        scratch_shapes=[
            pltpu.VMEM((N_GY, 5, 8, 128), F32),
            pltpu.VMEM((5, 8, 128), F32),
            pltpu.VMEM((N_GZ, 5, 8, 128), F32),
            pltpu.VMEM((N_GY, 5, 8, 128), F32),
            pltpu.VMEM((N_GZ, N_GY, 3, 128), F32),
            pltpu.VMEM((N_GY, N_GZ, 3, 128), F32),
        ]
        + [pltpu.SemaphoreType.DMA] * 10,
        compiler_params=pltpu.CompilerParams(collective_id=1, has_side_effects=True, vmem_limit_bytes=24 << 20),
    )(grads, ordered)


def on_device(velocity, wall_mask, hartmann_mask, tile_table, w_in, b_in, w_mid, b_mid, w_out, b_out):
    vel = velocity.reshape(ROWS, CZ)
    lo, hi, col = halo_call(vel, wall_mask)
    stepped, grads, ordered = main_call(
        vel, wall_mask, hartmann_mask, tile_table.reshape(TILES), lo, hi, col,
        w_in, b_in.reshape(1, HID), w_mid, b_mid.reshape(1, HID), w_out, b_out,
    )
    prediction, loss, grad_in, grad_bin, grad_mid, grad_bmid, grad_out, last = share_call(
        grads, ordered.reshape(N_GY, N_GZ, 3, 128)
    )
    return (
        stepped.reshape(3, STATIONS, CY, CZ),
        prediction,
        loss[0, 0],
        grad_in,
        grad_bin.reshape(HID),
        grad_mid,
        grad_bmid.reshape(HID),
        grad_out,
        last[0, 8:14],
    )


def solution(mesh):
    whole = P()
    in_specs = (P(None, None, "gy", "gz"), P("gy", "gz"), P("gy", "gz"), P(None, "gy", "gz")) + (whole,) * 6
    out_specs = (P(None, None, "gy", "gz"), P(None, ("gy", "gz"))) + (whole,) * 7
    return jax.shard_map(on_device, mesh=mesh, in_specs=in_specs, out_specs=out_specs, check_vma=False)
```

time: 536 us -> 93.3 us (0.17); the launches traced: 525 us -> 93 us
  local copies, waits for them, and re-layouts: 206 us -> 9.57 us
  waiting for transfers between devices: 102 us -> 0 us
  Pallas kernels: 0 us -> 81.4 us
  blocking collectives: 64 us -> 0 us
  matrix products: 59.1 us -> 0 us
  other arithmetic: 51.8 us -> 0 us
  starting transfers between devices: 25.7 us -> 0 us
  between operations: 16.7 us -> 1.96 us
    reshape x5 -> x1, local copies, waits for them, and re-layouts: 108 us -> 0.82 us  [on_device(): tile_table.reshape(TILES)]
    pallas_call x0 -> x3, Pallas kernels: none -> 81.4 us  [the longest x1 37.7 us: main_call(): pl.pallas_call(main_kernel, name='step_train', out_shape=[jax.ShapeDtypeS...]
    psum x1 -> x0, waiting for transfers between devices: 64.9 us -> none  [on_device(): lax.psum((grad_w_in, grad_b_in, grad_w_mid, grad_b_mid, grad_w_out, grad_...]
    psum x1 -> x0, blocking collectives: 64 us -> none  [on_device(): lax.psum((grad_w_in, grad_b_in, grad_w_mid, grad_b_mid, grad_w_out, grad_...]
    dot_general x16 -> x0, matrix products: 59.1 us -> none  [the longest x6 21.1 us: assemble(): jnp.dot(values[:, left_comp] * values[:, right_comp], point_pool, precisi...]
    all_to_all x1 -> x0, waiting for transfers between devices: 37 us -> none  [on_device(): lax.all_to_all(ordered, ('gy', 'gz'), split_axis=0, concat_axis=0, tiled=...]
    slice x6 -> x0, local copies, waits for them, and re-layouts: 29 us -> none  [the longest x2 16.3 us: extended(): head = lax.slice_in_dim(cells, 0, width, axis=dim)]
    unnamed x34 -> x25, local copies, waits for them, and re-layouts: 36.8 us -> 8.17 us
  transfers between devices with their start and end apart: 6 -> 0, of which waited for: 2 -> 0; matrix products, arithmetic and copies ran while one was open for 7% -> 0% of each run, Pallas kernels for 0% -> 0%
where the time goes in v1:
time: 93.3 us; the launch traced here: 93 us
  Pallas kernels  81.4 us (87%)
  local copies, waits for them, and re-layouts  9.57 us (10%)
  between operations  1.96 us (2%)
    pallas_call x1, Pallas kernels, main_call(): pl.pallas_call(main_kernel, name='step_train', out_shape=[jax.ShapeDtypeS...  37.7 us
    pallas_call x1, Pallas kernels, share_call(): pl.pallas_call(share_kernel, name='share', out_shape=[jax.ShapeDtypeStruc...  22.9 us
    pallas_call x1, Pallas kernels, halo_call(): pl.pallas_call(halo_kernel, name='halo', out_shape=[jax.ShapeDtypeStruct(...  20.8 us
    unnamed x25, local copies, waits for them, and re-layouts  8.17 us

profile of v1, /device:TPU:1, one launch (start us, length us, event | category | flops | bytes accessed | tf_op | source)
XLA Modules:
  0.0 93.0 jit_solution(16836422615217015301)
XLA Ops:
  0.6 0.0 copy-start.3
  0.7 0.0 copy-start.8
  0.7 0.0 copy-start.5
  0.7 0.0 copy-start.7
  0.7 0.0 copy-start.6
  0.7 0.0 copy-start.4
  0.7 0.8 reshape.43.table
  1.5 0.8 copy.19.w_in
  2.4 0.0 copy-start
  2.4 2.8 %copy-done = f32[3,128,32,128]{3,2,1,0:T(8,128)S(1)} copy-done((f32[3,128,32,128]{3,2,1,0:T(8,128)S(1)}, f32[3,128,32,128]{3,2,1,0:T(8,128)}, u32[]{:S(2)}) %copy-start) | copy-done | bytes 6291480
  5.1 0.0 copy-start.2
  5.2 0.7 copy-done.2
  5.9 0.0 copy-start.1
  5.9 20.8 %halo.1 = (f32[384,128]{1,0:T(8,128)S(1)}, f32[384,128]{1,0:T(8,128)S(1)}, f32[192,128]{1,0:T(8,128)S(1)}) custom-call(f32[12288,128]{1,0:T(8,128)S(1)} %bitcast.12, s32[32,128]{1,0:T(8,128)S(1)} %copy-done.2), custom_call_target="tpu_custom_call" | custom-call | tf_op jit(solution)/shard_map/halo/pallas_call | solution.py:105
  26.7 0.0 copy-done.3
  26.7 0.0 copy-done.8
  26.7 0.0 copy-done.5
  26.7 0.0 copy-done.7
  26.8 0.0 copy-done.6
  26.8 0.0 copy-done.4
  26.8 0.0 copy-done.1
  26.8 37.7 %step_train.1 = (bf16[12288,128]{1,0:T(8,128)(2,1)}, f32[16,5,8,128]{3,2,1,0:T(8,128)S(1)}, f32[128,3,128]{2,1,0:T(4,128)S(1)}) custom-call(f32[12288,128]{1,0:T(8,128)} %bitcast.11, s32[32,128]{1,0:T(8,128)S(1)} %copy-done.3, s32[32,128]{1,0:T(8,128)S(1)} %copy-done.4, s32[128]{0:T(128)S(1)} %reshape.43.table, f32[384,128]{1,0:T(8,128)S(1)} %get-tuple-element.23.lo, ...), custom_call_target="tpu_custom_call" | custom-call | tf_op jit(solution)/shard_map/step_train/pallas_call | solution.py:381
  64.5 22.9 %share.1 = (f32[6,8192]{1,0:T(8,128)S(1)}, f32[1,128]{1,0:T(1,128)S(1)}, f32[256,24]{1,0:T(8,128)S(1)}, f32[1,256]{1,0:T(1,128)S(1)}, f32[256,256]{1,0:T(8,128)S...) custom-call(f32[16,5,8,128]{3,2,1,0:T(8,128)S(1)} %get-tuple-element.27.g, ...), custom_call_target="tpu_custom_call" | custom-call | tf_op jit(solution)/shard_map/share/pallas_call | solution.py:492
  87.4 0.6 slice_bitcast_fusion
  88.0 0.7 copy.20
  88.7 0.7 copy.27
  89.4 0.6 copy.29
  90.0 0.7 copy.30
  90.7 0.6 copy.31
  91.2 0.6 copy.32
Async XLA Ops:
  0.6 26.1 %copy-start.3 = (s32[32,128]{1,0:T(8,128)S(1)}, s32[32,128]{1,0:T(8,128)}, u32[]{:S(2)}) copy-start(s32[32,128]{1,0:T(8,128)} %wall.3) | copy-start | bytes 49156
  0.7 26.1 %copy-start.8 = (f32[6]{0:T(128)S(1)}, f32[6]{0:T(128)}, u32[]{:S(2)}) copy-start(f32[6]{0:T(128)} %b_out.1) | copy-start | bytes 76
  0.7 26.1 %copy-start.5 = (bf16[6,256]{1,0:T(8,128)(2,1)S(1)}, bf16[6,256]{1,0:T(8,128)(2,1)}, u32[]{:S(2)}) copy-start(bf16[6,256]{1,0:T(8,128)(2,1)} %w_out.1) | copy-start | bytes 9220
  0.7 26.1 %copy-start.7 = (f32[256]{0:T(256)S(1)}, f32[256]{0:T(256)}, u32[]{:S(2)}) copy-start(f32[256]{0:T(256)} %param.17) | copy-start | bytes 3076
  0.7 26.1 %copy-start.6 = (f32[256]{0:T(256)S(1)}, f32[256]{0:T(256)}, u32[]{:S(2)}) copy-start(f32[256]{0:T(256)} %param.15) | copy-start | bytes 3076
  0.7 26.1 %copy-start.4 = (s32[32,128]{1,0:T(8,128)S(1)}, s32[32,128]{1,0:T(8,128)}, u32[]{:S(2)}) copy-start(s32[32,128]{1,0:T(8,128)} %hart.1) | copy-start | bytes 49156
  2.4 2.8 %copy-start = (f32[3,128,32,128]{3,2,1,0:T(8,128)S(1)}, f32[3,128,32,128]{3,2,1,0:T(8,128)}, u32[]{:S(2)}) copy-start(f32[3,128,32,128]{3,2,1,0:T(8,128)} %param.10) | copy-start | bytes 18874372
  5.1 0.7 copy-start.2
  5.9 20.9 %copy-start.1 = (bf16[256,256]{1,0:T(8,128)(2,1)S(1)}, bf16[256,256]{1,0:T(8,128)(2,1)}, u32[]{:S(2)}) copy-start(bf16[256,256]{1,0:T(8,128)(2,1)} %w_mid.1) | copy-start | bytes 393220

commit v2 on v1

--- a/solution.py
+++ b/solution.py
@@ -19,7 +19,6 @@
 ROWS = 3 * STATIONS * CY
 SLABS = 8
 LANES = 1024
-PART = 512
 F32 = jnp.float32
 BF16 = jnp.bfloat16
 PAIRS = ((0, 0), (1, 1), (2, 2), (0, 1), (0, 2), (1, 2))
@@ -34,55 +33,58 @@
     pltpu.make_async_copy(ref, ref, sem).wait()
 
 
-def pack_edges(v, fluid, edge_lo, edge_hi, columns):
+def pack_edges(v, fluid, edge_lo, edge_hi):
     for c in range(3):
         first = c * STATIONS * CY
-        edge_lo[pl.ds(c * STATIONS, STATIONS), :] = v[pl.ds(first, STATIONS, stride=CY), :] * fluid[0:1, :]
-        edge_hi[pl.ds(c * STATIONS, STATIONS), :] = (
-            v[pl.ds(first + CY - 1, STATIONS, stride=CY), :] * fluid[CY - 1 : CY, :]
-        )
+        rows = pl.ds(c * STATIONS, STATIONS)
+        edge_lo[rows, :] = (v[pl.ds(first, STATIONS, stride=CY), :] * fluid[0:1, :]).astype(BF16)
+        edge_hi[rows, :] = (v[pl.ds(first + CY - 1, STATIONS, stride=CY), :] * fluid[CY - 1 : CY, :]).astype(BF16)
+
+
+def pack_columns(v, fluid, to_left, to_right):
     pair = iota((8, 128), 1) // 2
-
-    def station(s, acc):
-        here = pair == s
-        out = []
-        for c in range(3):
+    odd = iota((8, 128), 1) % 2 == 1
+    for c in range(3):
+
+        def station(s, acc):
+            here = pair == s
+            out = []
             for h in range(2):
                 for j in range(4):
                     cells = v[pl.ds((c * STATIONS + h * 64 + s) * CY + 8 * j, 8), :]
-                    moved = pltpu.roll(cells, 2 * s + 1, 1)
-                    out.append(jnp.where(here, moved, acc[len(out)]))
-        return tuple(out)
-
-    packed = lax.fori_loop(0, 64, station, tuple(jnp.zeros((8, 128), F32) for _ in range(24)))
-    odd = iota((8, 128), 1) % 2 == 1
-    for c in range(3):
-        for h in range(2):
-            for j in range(4):
+                    out.append(jnp.where(here, pltpu.roll(cells, 2 * s + 1, 1), acc[len(out)]))
+            return tuple(out)
+
+        packed = lax.fori_loop(0, 64, station, tuple(jnp.zeros((8, 128), F32) for _ in range(8)), unroll=8)
+        for k in range(2):
+            left, right = [], []
+            for j in (2 * k, 2 * k + 1):
                 mask = fluid[8 * j : 8 * j + 8, :]
-                ends = jnp.where(odd, mask[:, 0:1], mask[:, CZ - 1 : CZ])
-                columns[pl.ds((c * 2 + h) * CY + 8 * j, 8), :] = packed[(c * 2 + h) * 4 + j] * ends
-
-
-def halo_kernel(vel, wall, lo_out, hi_out, col_out, v, fluid, edge_lo, edge_hi, columns, got_lo, got_hi, got_left, got_right, load, send, recv):
+                near, far = packed[j], packed[4 + j]
+                right.append(jnp.where(odd, pltpu.roll(far, 1, 1), near) * mask[:, CZ - 1 : CZ])
+                left.append(jnp.where(odd, far, pltpu.roll(near, 127, 1)) * mask[:, 0:1])
+            rows = pl.ds(c * CY + 16 * k, 16)
+            to_right[rows, :] = jnp.concatenate(right, axis=0).astype(BF16)
+            to_left[rows, :] = jnp.concatenate(left, axis=0).astype(BF16)
+
+
+def halo_kernel(v, wall, lo_out, hi_out, col_out, fluid, edge_lo, edge_hi, to_left, to_right, got_lo, got_hi, got_left, got_right, send, recv):
     y = lax.axis_index("gy")
     z = lax.axis_index("gz")
     below = ((y + N_GY - 1) % N_GY, z)
     above = ((y + 1) % N_GY, z)
     left = (y, (z + N_GZ - 1) % N_GZ)
     right = (y, (z + 1) % N_GZ)
-    fetch = pltpu.make_async_copy(vel, v, load)
-    fetch.start()
     barrier = pltpu.get_barrier_semaphore()
     for peer in (below, above, left, right):
         pl.semaphore_signal(barrier, inc=1, device_id=peer, device_id_type=MESH)
     fluid[...] = (1 - wall[...]).astype(F32)
-    fetch.wait()
-    pack_edges(v, fluid, edge_lo, edge_hi, columns)
+    pack_columns(v, fluid, to_left, to_right)
+    pack_edges(v, fluid, edge_lo, edge_hi)
     pl.semaphore_wait(barrier, 4)
     copies = []
     for k, (src, dst, peer) in enumerate(
-        ((edge_lo, got_hi, below), (edge_hi, got_lo, above), (columns, got_right, left), (columns, got_left, right))
+        ((to_left, got_right, left), (to_right, got_left, right), (edge_lo, got_hi, below), (edge_hi, got_lo, above))
     ):
         copy = pltpu.make_async_remote_copy(
             src, dst, send.at[k], recv.at[k], device_id=peer, device_id_type=MESH
@@ -90,18 +92,27 @@
         copy.start()
         copies.append(copy)
     for copy in copies:
-        copy.wait()
-    lo_out[...] = got_lo[...] * jnp.where(y > 0, 1.0, 0.0)
-    hi_out[...] = got_hi[...] * jnp.where(y < N_GY - 1, 1.0, 0.0)
+        copy.wait_recv()
+    lo_out[...] = got_lo[...].astype(F32) * jnp.where(y > 0, 1.0, 0.0)
+    hi_out[...] = got_hi[...].astype(F32) * jnp.where(y < N_GY - 1, 1.0, 0.0)
     has_left = jnp.where(z > 0, 1.0, 0.0)
     has_right = jnp.where(z < N_GZ - 1, 1.0, 0.0)
-    odd = iota((8, 128), 1) % 2 == 1
-    for k in range(24):
-        rows = pl.ds(8 * k, 8)
-        col_out[rows, :] = jnp.where(odd, got_right[rows, :] * has_right, pltpu.roll(got_left[rows, :] * has_left, 2, 1))
+    odd = iota((16, 128), 1) % 2 == 1
+    for c in range(3):
+        for k in range(2):
+            rows = pl.ds(c * CY + 16 * k, 16)
+            lower = got_left[rows, :].astype(F32) * has_left
+            upper = got_right[rows, :].astype(F32) * has_right
+            near = jnp.where(odd, pltpu.roll(upper, 1, 1), pltpu.roll(lower, 2, 1))
+            far = jnp.where(odd, upper, pltpu.roll(lower, 1, 1))
+            col_out[pl.ds((c * 2) * CY + 16 * k, 16), :] = near
+            col_out[pl.ds((c * 2 + 1) * CY + 16 * k, 16), :] = far
+    for copy in copies:
+        copy.wait_send()
 
 
 def halo_call(vel, wall):
+    vm = pl.BlockSpec(memory_space=pltpu.VMEM)
     return pl.pallas_call(
         halo_kernel,
         name="halo",
@@ -110,23 +121,22 @@
             jax.ShapeDtypeStruct((384, 128), F32),
             jax.ShapeDtypeStruct((192, 128), F32),
         ],
-        in_specs=[pl.BlockSpec(memory_space=pl.ANY), pl.BlockSpec(memory_space=pltpu.VMEM)],
-        out_specs=[pl.BlockSpec(memory_space=pltpu.VMEM)] * 3,
+        in_specs=[vm, vm],
+        out_specs=[vm] * 3,
         scratch_shapes=[
-            pltpu.VMEM((ROWS, 128), F32),
             pltpu.VMEM((CY, 128), F32),
-            pltpu.VMEM((384, 128), F32),
-            pltpu.VMEM((384, 128), F32),
-            pltpu.VMEM((192, 128), F32),
-            pltpu.VMEM((384, 128), F32),
-            pltpu.VMEM((384, 128), F32),
-            pltpu.VMEM((192, 128), F32),
-            pltpu.VMEM((192, 128), F32),
-            pltpu.SemaphoreType.DMA,
+            pltpu.VMEM((384, 128), BF16),
+            pltpu.VMEM((384, 128), BF16),
+            pltpu.VMEM((96, 128), BF16),
+            pltpu.VMEM((96, 128), BF16),
+            pltpu.VMEM((384, 128), BF16),
+            pltpu.VMEM((384, 128), BF16),
+            pltpu.VMEM((96, 128), BF16),
+            pltpu.VMEM((96, 128), BF16),
             pltpu.SemaphoreType.DMA((4,)),
             pltpu.SemaphoreType.DMA((4,)),
         ],
-        compiler_params=pltpu.CompilerParams(collective_id=0, has_side_effects=True, vmem_limit_bytes=24 << 20),
+        compiler_params=pltpu.CompilerParams(collective_id=0, has_side_effects=True, vmem_limit_bytes=16 << 20),
     )(vel, wall)
 
 
@@ -219,9 +229,12 @@
     lane = iota((HID, 128), 1)
     bias = column_table(b_in[...]) * 0.5
     high = bias.astype(BF16).astype(F32)
-    tmp[...] = jnp.zeros_like(tmp)
-    tmp[:, 0:24] = w_in[...].astype(F32) * 0.5
-    full = tmp[...]
+    tmp[pl.ds(0, 128), :] = jnp.zeros((128, 128), F32)
+    halves = []
+    for h in range(2):
+        tmp[pl.ds(0, 24), :] = w_in[:, 128 * h : 128 * h + 128].astype(F32) * 0.5
+        halves.append(jnp.transpose(tmp[pl.ds(0, 128), :]))
+    full = jnp.concatenate(halves, axis=0)
     full = jnp.where(lane == 30, high, jnp.where(lane == 31, bias - high, full))
     win[...] = full[:, 0:32].astype(BF16)
     mid = w_mid[...].astype(F32) * 0.5
@@ -278,7 +291,7 @@
     g_mid[...] += lax.dot_general(grad2, act1, NT, preferred_element_type=F32)
     d1 = jnp.dot(wmid_t[...], grad2, preferred_element_type=F32) * slope1
     grad1 = d1.astype(BF16)
-    g_in[...] += lax.dot_general(x, grad1, NT, preferred_element_type=F32)
+    g_in[...] += lax.dot_general(grad1, x, NT, preferred_element_type=F32)
 
 
 def scatter_slab(a, pred, table, ordered):
@@ -295,29 +308,19 @@
             for q in range(1, 4):
                 value = jnp.where(quarter == q, jnp.take_along_axis(blocks[q], index, axis=1), value)
             value = jnp.where(low, value, pltpu.roll(value, 5, 0))
-            ordered[table[a * 16 + b * 8 + c]] = value[0:3]
+            ordered[table[a, b, c]] = value[0:3]
 
 
 def main_kernel(
-    vel, wall, hart, table, lo, hi, col, w_in, b_in, w_mid, b_mid, w_out, b_out,
+    v, wall, hart, table, lo, hi, col, w_in, b_in, w_mid, b_mid, w_out, b_out,
     stepped_out, grads, ordered,
-    v, stepped, rounded, tables, feat, xs, targets, pred, win, wmid, wmid_t, wout, wout_t, bias_mid, bias_out, tmp,
-    g_in, g_mid, g_out, g_bmid, g_bout, g_loss, load, store,
+    stepped, rounded, tables, feat, xs, targets, pred, win, wmid, wmid_t, wout, wout_t, bias_mid, bias_out, tmp,
+    g_in, g_mid, g_out, g_bmid, g_bout, g_loss, store,
 ):
-    def fetch(c, i):
-        rows = pl.ds(c * STATIONS * CY + i * 16 * CY, 16 * CY)
-        return pltpu.make_async_copy(vel.at[rows], v.at[rows], load.at[i])
-
-    def fetches(i, act):
-        for c in range(3):
-            getattr(fetch(c, i), act)()
-
     def store_copy(c, a):
         rows = pl.ds(pl.multiple_of(c * STATIONS * CY + a * 16 * CY, 16), 16 * CY)
         return pltpu.make_async_copy(stepped.at[rows], stepped_out.at[rows], store.at[c])
 
-    for i in (7, 0, 1, 2, 3, 4, 5, 6):
-        fetches(i, "start")
     fluid = (1 - wall[...]).astype(F32)
     tables[pl.ds(0, 32), :] = fluid
     tables[pl.ds(32, 32), :] = fluid * 0.1
@@ -326,39 +329,50 @@
     for ref in (g_in, g_mid, g_out, g_bmid, g_bout, g_loss):
         ref[...] = jnp.zeros_like(ref)
     feat[pl.ds(240, 16), :] = jnp.ones((16, 128), F32)
-    for i in (7, 0, 1, 2, 3, 4, 5, 6):
-        fetches(i, "wait")
-
-    def slab(a, carry):
-        def station(s, inner):
+
+    def stencil_slab(a):
+        def station(s):
             stencil_station(v, lo, hi, col, tables, stepped, rounded, a * 16 + s, s)
-            return inner
-
-        lax.fori_loop(0, 16, station, 0)
+
+        for s in range(16):
+            station(s)
         for c in range(3):
             store_copy(c, a).start()
+
+    def samples(a):
         pool_slab(rounded, feat)
         for yp in range(8):
             lanes = slice(128 * yp, 128 * yp + 128)
             xs[:, lanes] = feat[pl.ds(yp, 32, stride=8), :].astype(BF16)
             targets[:, lanes] = feat[pl.ds(192 + yp, 8, stride=8), :]
-        for k in range(LANES // PART):
-            lanes = slice(PART * k, PART * k + PART)
-            train_part(
-                xs[:, lanes], targets[:, lanes], win, wmid, wmid_t, wout, wout_t, bias_mid, bias_out,
-                pred.at[:, lanes], g_in, g_mid, g_out, g_bmid, g_bout, g_loss,
-            )
+
+    def train(a):
+        train_part(
+            xs[...], targets[...], win, wmid, wmid_t, wout, wout_t, bias_mid, bias_out,
+            pred, g_in, g_mid, g_out, g_bmid, g_bout, g_loss,
+        )
         scatter_slab(a, pred, table, ordered)
+
+    def slab(a, carry):
+        samples(a)
+        train(a)
+        stencil_slab(a + 1)
         return carry
 
-    lax.fori_loop(0, SLABS, slab, 0)
+    stencil_slab(0)
+    lax.fori_loop(0, SLABS - 1, slab, 0)
+    samples(SLABS - 1)
+    train(SLABS - 1)
     for c in range(3):
         wait_bytes(stepped.at[pl.ds(0, STATIONS * CY)], store.at[c])
     for t in range(64):
         grads[t // 5, t % 5] = g_mid[pl.ds(8 * (t // 2), 8), 128 * (t % 2) : 128 * (t % 2) + 128]
-    for k in range(8):
-        t = 64 + k
-        grads[t // 5, t % 5] = g_in[pl.ds(8 * (k // 2), 8), 128 * (k % 2) : 128 * (k % 2) + 128]
+    tmp[:, 0:32] = g_in[...]
+    for h in range(2):
+        turned = jnp.transpose(tmp[pl.ds(128 * h, 128), :])
+        for k in range(4):
+            t = 64 + 2 * k + h
+            grads[t // 5, t % 5] = turned[8 * k : 8 * k + 8]
     row = iota((8, 128), 0)
     lane = iota((8, 128), 1)
     sums_out = jnp.sum(g_bout[...], axis=1, keepdims=True)
@@ -386,10 +400,9 @@
             jax.ShapeDtypeStruct((16, 5, 8, 128), F32),
             jax.ShapeDtypeStruct((TILES, 3, 128), F32),
         ],
-        in_specs=[anywhere, vm, vm, sm, vm, vm, vm, vm, vm, vm, vm, vm, sm],
+        in_specs=[vm, vm, vm, sm, vm, vm, vm, vm, vm, vm, vm, vm, sm],
         out_specs=[anywhere, vm, vm],
         scratch_shapes=[
-            pltpu.VMEM((ROWS, 128), F32),
             pltpu.VMEM((ROWS, 128), BF16),
             pltpu.VMEM((3 * 16 * CY, 128), F32),
             pltpu.VMEM((96, 128), F32),
@@ -405,22 +418,21 @@
             pltpu.VMEM((HID, 128), F32),
             pltpu.VMEM((8, 128), F32),
             pltpu.VMEM((HID, 128), F32),
-            pltpu.VMEM((32, HID), F32),
+            pltpu.VMEM((HID, 32), F32),
             pltpu.VMEM((HID, HID), F32),
             pltpu.VMEM((16, HID), F32),
             pltpu.VMEM((HID, 128), F32),
             pltpu.VMEM((8, 128), F32),
             pltpu.VMEM((8, 128), F32),
-            pltpu.SemaphoreType.DMA((8,)),
             pltpu.SemaphoreType.DMA((3,)),
         ],
-        compiler_params=pltpu.CompilerParams(vmem_limit_bytes=48 << 20),
+        compiler_params=pltpu.CompilerParams(vmem_limit_bytes=32 << 20),
     )(vel, wall, hart, table, lo, hi, col, w_in, b_in, w_mid, b_mid, w_out, b_out)
 
 
 def share_kernel(
-    g, p, pred_out, loss_out, in_out, bin_out, mid_out, bmid_out, out_out, bout_out,
-    part, mine, column, total, hop, got, s0, r0, s1, r1, s2, r2, s3, r3, s4, r4,
+    g, p, total, got,
+    part, mine, column, hop, s0, r0, s1, r1, s2, r2, s3, r3, s4, r4,
 ):
     y = lax.axis_index("gy")
     z = lax.axis_index("gz")
@@ -459,6 +471,37 @@
         send(mine, total.at[y], s4, r4, q, z)
     total[y] = mine[...]
     wait_bytes(got.at[pl.ds(0, N_GY - 1)], r3)
+    wait_bytes(total.at[pl.ds(0, N_GY - 1)], r4)
+    wait_bytes(part.at[pl.ds(0, N_GY - 1)], s0)
+    wait_bytes(hop.at[pl.ds(0, N_GZ - 1)], s1)
+    wait_bytes(column.at[pl.ds(0, N_GZ - 1)], s2)
+    wait_bytes(got.at[pl.ds(0, N_GY - 1)], s3)
+    wait_bytes(total.at[pl.ds(0, N_GY - 1)], s4)
+
+
+def share_call(grads, ordered):
+    vm = pl.BlockSpec(memory_space=pltpu.VMEM)
+    return pl.pallas_call(
+        share_kernel,
+        name="share",
+        out_shape=[
+            jax.ShapeDtypeStruct((N_GY, 5, 8, 128), F32),
+            jax.ShapeDtypeStruct((N_GY, N_GZ, 3, 128), F32),
+        ],
+        in_specs=[vm, vm],
+        out_specs=[vm] * 2,
+        scratch_shapes=[
+            pltpu.VMEM((N_GY, 5, 8, 128), F32),
+            pltpu.VMEM((5, 8, 128), F32),
+            pltpu.VMEM((N_GZ, 5, 8, 128), F32),
+            pltpu.VMEM((N_GZ, N_GY, 3, 128), F32),
+        ]
+        + [pltpu.SemaphoreType.DMA] * 10,
+        compiler_params=pltpu.CompilerParams(collective_id=1, has_side_effects=True, vmem_limit_bytes=16 << 20),
+    )(grads, ordered)
+
+
+def finish_kernel(total, got, pred_out, loss_out, in_out, bin_out, mid_out, bmid_out, out_out, bout_out):
     low = iota((3, 128), 1) < 64
     for j in range(TILES // 2):
         first = got[(2 * j) // N_GZ, (2 * j) % N_GZ]
@@ -466,77 +509,64 @@
         lanes = slice(128 * j, 128 * j + 128)
         pred_out[0:3, lanes] = jnp.where(low, first, pltpu.roll(second, 64, 1))
         pred_out[3:6, lanes] = jnp.where(low, pltpu.roll(first, 64, 1), second)
-    wait_bytes(total.at[pl.ds(0, N_GY - 1)], r4)
     for t in range(64):
         mid_out[pl.ds(8 * (t // 2), 8), 128 * (t % 2) : 128 * (t % 2) + 128] = total[t // 5, t % 5]
     for h in range(2):
-        rows = jnp.concatenate([total[(64 + 2 * k + h) // 5, (64 + 2 * k + h) % 5] for k in range(4)], axis=0)
-        padded = jnp.concatenate([rows, jnp.zeros((96, 128), F32)], axis=0)
-        in_out[pl.ds(128 * h, 128), :] = jnp.transpose(padded)[:, 0:24]
-        bin_out[:, 128 * h : 128 * h + 128] = rows[30:31]
+        lanes = slice(128 * h, 128 * h + 128)
+        for k in range(4):
+            t = 64 + 2 * k + h
+            if k < 3:
+                in_out[pl.ds(8 * k, 8), lanes] = total[t // 5, t % 5]
+            else:
+                bin_out[:, lanes] = total[t // 5, t % 5][6:7]
         last = total[(72 + h) // 5, (72 + h) % 5]
-        out_out[:, 128 * h : 128 * h + 128] = last[0:6]
-        bmid_out[:, 128 * h : 128 * h + 128] = last[6:7]
+        out_out[:, lanes] = last[0:6]
+        bmid_out[:, lanes] = last[6:7]
         if h == 0:
-            loss_out[...] = last[7:8] * (1.0 / (6 * SAMPLES))
-            bout_out[...] = last[7:8]
-    wait_bytes(part.at[pl.ds(0, N_GY - 1)], s0)
-    wait_bytes(hop.at[pl.ds(0, N_GZ - 1)], s1)
-    wait_bytes(column.at[pl.ds(0, N_GZ - 1)], s2)
-    wait_bytes(got.at[pl.ds(0, N_GY - 1)], s3)
-    wait_bytes(total.at[pl.ds(0, N_GY - 1)], s4)
-
-
-def share_call(grads, ordered):
+            loss_out[...] = last[7:8, 0:1] * (1.0 / (6 * SAMPLES))
+            bout_out[...] = pltpu.roll(last, 120, 1)[7:8, 0:6]
+
+
+def finish_call(total, got):
     vm = pl.BlockSpec(memory_space=pltpu.VMEM)
     return pl.pallas_call(
-        share_kernel,
-        name="share",
+        finish_kernel,
+        name="finish",
         out_shape=[
             jax.ShapeDtypeStruct((6, 64 * 128), F32),
-            jax.ShapeDtypeStruct((1, 128), F32),
-            jax.ShapeDtypeStruct((HID, 24), F32),
+            jax.ShapeDtypeStruct((1, 1), F32),
+            jax.ShapeDtypeStruct((24, HID), F32),
             jax.ShapeDtypeStruct((1, HID), F32),
             jax.ShapeDtypeStruct((HID, HID), F32),
             jax.ShapeDtypeStruct((1, HID), F32),
             jax.ShapeDtypeStruct((6, HID), F32),
-            jax.ShapeDtypeStruct((1, 128), F32),
+            jax.ShapeDtypeStruct((1, 6), F32),
         ],
         in_specs=[vm, vm],
         out_specs=[vm] * 8,
-        scratch_shapes=[
-            pltpu.VMEM((N_GY, 5, 8, 128), F32),
-            pltpu.VMEM((5, 8, 128), F32),
-            pltpu.VMEM((N_GZ, 5, 8, 128), F32),
-            pltpu.VMEM((N_GY, 5, 8, 128), F32),
-            pltpu.VMEM((N_GZ, N_GY, 3, 128), F32),
-            pltpu.VMEM((N_GY, N_GZ, 3, 128), F32),
-        ]
-        + [pltpu.SemaphoreType.DMA] * 10,
-        compiler_params=pltpu.CompilerParams(collective_id=1, has_side_effects=True, vmem_limit_bytes=24 << 20),
-    )(grads, ordered)
+        compiler_params=pltpu.CompilerParams(vmem_limit_bytes=16 << 20),
+    )(total, got)
 
 
 def on_device(velocity, wall_mask, hartmann_mask, tile_table, w_in, b_in, w_mid, b_mid, w_out, b_out):
     vel = velocity.reshape(ROWS, CZ)
     lo, hi, col = halo_call(vel, wall_mask)
     stepped, grads, ordered = main_call(
-        vel, wall_mask, hartmann_mask, tile_table.reshape(TILES), lo, hi, col,
-        w_in, b_in.reshape(1, HID), w_mid, b_mid.reshape(1, HID), w_out, b_out,
+        vel, wall_mask, hartmann_mask, tile_table, lo, hi, col,
+        w_in.T, b_in.reshape(1, HID), w_mid, b_mid.reshape(1, HID), w_out, b_out,
     )
-    prediction, loss, grad_in, grad_bin, grad_mid, grad_bmid, grad_out, last = share_call(
-        grads, ordered.reshape(N_GY, N_GZ, 3, 128)
-    )
+    total, got = share_call(grads, ordered.reshape(N_GY, N_GZ, 3, 128))
+    prediction, loss, grad_in, grad_bin, grad_mid, grad_bmid, grad_out, grad_bout = finish_call(total, got)
     return (
         stepped.reshape(3, STATIONS, CY, CZ),
         prediction,
-        loss[0, 0],
-        grad_in,
+        loss.reshape(()),
+        grad_in.T,
         grad_bin.reshape(HID),
         grad_mid,
         grad_bmid.reshape(HID),
         grad_out,
-        last[0, 8:14],
+        grad_bout.reshape(6),
     )
 
 

time: 93.3 us -> 62.1 us (0.67)
  Pallas kernels: 81.4 us -> 55.2 us
  local copies, waits for them, and re-layouts: 9.57 us -> 5.84 us
  between operations: 1.96 us -> 0.77 us
    pallas_call x1, Pallas kernels: 37.7 us -> 18.9 us  [main_call(): pl.pallas_call(main_kernel, name='step_train', out_shape=[jax.ShapeDtypeS...]
    pallas_call x1, Pallas kernels: 20.8 us -> 12.6 us  [halo_call(): pl.pallas_call(halo_kernel, name='halo', out_shape=[jax.ShapeDtypeStruct(...]
    unnamed x25 -> x22, local copies, waits for them, and re-layouts: 8.17 us -> 5.84 us
    pallas_call x0 -> x1, Pallas kernels: none -> 0.95 us  [finish_call(): pl.pallas_call(finish_kernel, name='finish', out_shape=[jax.ShapeDtypeStr...]
where the time goes in v2:
time: 62.1 us; the launch traced here: 61.8 us
  Pallas kernels  55.2 us (89%)
  local copies, waits for them, and re-layouts  5.84 us (9%)
  between operations  0.77 us (1%)
    pallas_call x1, Pallas kernels, share_call(): pl.pallas_call(share_kernel, name='share', out_shape=[jax.ShapeDtypeStruc...  22.7 us
    pallas_call x1, Pallas kernels, main_call(): pl.pallas_call(main_kernel, name='step_train', out_shape=[jax.ShapeDtypeS...  18.9 us
    pallas_call x1, Pallas kernels, halo_call(): pl.pallas_call(halo_kernel, name='halo', out_shape=[jax.ShapeDtypeStruct(...  12.6 us
    unnamed x22, local copies, waits for them, and re-layouts  5.84 us

profile of v2, /device:TPU:1, one launch (start us, length us, event | category | flops | bytes accessed | tf_op | source)
XLA Modules:
  0.0 61.8 jit_solution(1164406864405459195)
XLA Ops:
  0.6 0.0 copy-start.10
  0.7 0.0 copy-start.7
  0.7 0.0 copy-start.9
  0.7 0.0 copy-start.8
  0.7 0.0 copy-start
  0.7 2.8 %copy-done = f32[3,128,32,128]{3,2,1,0:T(8,128)S(1)} copy-done((f32[3,128,32,128]{3,2,1,0:T(8,128)S(1)}, f32[3,128,32,128]{3,2,1,0:T(8,128)}, u32[]{:S(2)}) %copy-start) | copy-done | bytes 6291480
  3.5 0.0 copy-start.3
  3.5 0.7 %copy-done.3 = s32[32,128]{1,0:T(8,128)S(1)} copy-done((s32[32,128]{1,0:T(8,128)S(1)}, s32[32,128]{1,0:T(8,128)}, u32[]{:S(2)}) %copy-start.3) | copy-done | bytes 16408
  4.2 0.0 copy-start.1
  4.2 0.0 copy-start.4
  4.2 12.6 %halo.1 = (f32[384,128]{1,0:T(8,128)S(1)}, f32[384,128]{1,0:T(8,128)S(1)}, f32[192,128]{1,0:T(8,128)S(1)}) custom-call(f32[12288,128]{1,0:T(8,128)S(1)} %bitcast.11, s32[32,128]{1,0:T(8,128)S(1)} %copy-done.3), custom_call_target="tpu_custom_call" | custom-call | tf_op jit(solution)/shard_map/halo/pallas_call | solution.py:116
  16.8 0.0 copy-done.10
  16.8 0.0 copy-done.7
  16.8 0.0 copy-done.9
  16.8 0.0 copy-done.8
  16.8 0.0 copy-done.1
  16.8 0.0 copy-done.4
  16.9 0.0 copy-start.2
  16.9 0.9 %copy-done.2 = bf16[256,256]{1,0:T(8,128)(2,1)S(1)} copy-done((bf16[256,256]{1,0:T(8,128)(2,1)S(1)}, bf16[256,256]{1,0:T(8,128)(2,1)}, u32[]{:S(2)}) %copy-start.2) | copy-done | bytes 131096
  17.8 0.0 copy-start.5
  17.8 0.7 %copy-done.5 = bf16[256,24]{0,1:T(8,128)(2,1)S(1)} copy-done((bf16[256,24]{0,1:T(8,128)(2,1)S(1)}, bf16[256,24]{0,1:T(8,128)(2,1)}, u32[]{:S(2)}) %copy-start.5) | copy-done | bytes 12312
  18.5 0.0 copy-start.6
  18.5 0.7 %copy-done.6 = s32[8,2,8]{2,1,0:T(2,128)S(1)} copy-done((s32[8,2,8]{2,1,0:T(2,128)S(1)}, s32[8,2,8]{2,1,0:T(2,128)}, u32[]{:S(2)}) %copy-start.6) | copy-done | bytes 536
  19.2 18.9 %step_train.1 = (bf16[12288,128]{1,0:T(8,128)(2,1)}, f32[16,5,8,128]{3,2,1,0:T(8,128)S(1)}, f32[128,3,128]{2,1,0:T(4,128)S(1)}) custom-call(f32[12288,128]{1,0:T(8,128)S(1)} %bitcast.12, s32[32,128]{1,0:T(8,128)S(1)} %copy-done.3, s32[32,128]{1,0:T(8,128)S(1)} %copy-done.4, s32[8,2,8]{2,1,0:T(2,128)S(1)} %copy-done.6, f32[384,128]{1,0:T(8,128)S(1)} %get-tuple-element.25.lo, ...), custom_call_target="tpu_custom_call" | custom-call | tf_op jit(solution)/shard_map/step_train/pallas_call | solution.py:395
  38.1 22.7 %share.1 = (f32[16,5,8,128]{3,2,1,0:T(8,128)S(1)}, f32[16,8,3,128]{3,2,1,0:T(4,128)S(1)}) custom-call(f32[16,5,8,128]{3,2,1,0:T(8,128)S(1)} %get-tuple-element.29.g, f32[16,8,3,128]{3,2,1,0:T(4,128)S(1)} %bitcast.13), custom_call_target="tpu_custom_call" | custom-call | tf_op jit(solution)/shard_map/share/pallas_call | solution.py:484
  60.8 1.0 %finish.1 = (f32[6,8192]{1,0:T(8,128)}, f32[1,1]{1,0:T(1,128)}, f32[24,256]{1,0:T(8,128)}, f32[1,256]{1,0:T(1,128)}, f32[256,256]{1,0:T(8,128)}, /*index=5*/f32[...) custom-call(f32[16,5,8,128]{3,2,1,0:T(8,128)S(1)} %get-tuple-element.31.total, f32[16,8,3,128]{3,2,1,0:T(4,128)S(1)} %get-tuple-element.32.got), custom_call_target="tpu_custom_call" | custom-call | tf_op jit(solution)/shard_map/finish/pallas_call | solution.py:532
Async XLA Ops:
  0.6 16.2 %copy-start.10 = (f32[6]{0:T(128)S(1)}, f32[6]{0:T(128)}, u32[]{:S(2)}) copy-start(f32[6]{0:T(128)} %b_out.1) | copy-start | bytes 76
  0.7 16.2 %copy-start.7 = (bf16[6,256]{1,0:T(8,128)(2,1)S(1)}, bf16[6,256]{1,0:T(8,128)(2,1)}, u32[]{:S(2)}) copy-start(bf16[6,256]{1,0:T(8,128)(2,1)} %w_out.1) | copy-start | bytes 9220
  0.7 16.2 %copy-start.9 = (f32[256]{0:T(256)S(1)}, f32[256]{0:T(256)}, u32[]{:S(2)}) copy-start(f32[256]{0:T(256)} %param.17) | copy-start | bytes 3076
  0.7 16.2 %copy-start.8 = (f32[256]{0:T(256)S(1)}, f32[256]{0:T(256)}, u32[]{:S(2)}) copy-start(f32[256]{0:T(256)} %param.15) | copy-start | bytes 3076
  0.7 2.8 %copy-start = (f32[3,128,32,128]{3,2,1,0:T(8,128)S(1)}, f32[3,128,32,128]{3,2,1,0:T(8,128)}, u32[]{:S(2)}) copy-start(f32[3,128,32,128]{3,2,1,0:T(8,128)} %param.10) | copy-start | bytes 18874372
  3.5 0.7 %copy-start.3 = (s32[32,128]{1,0:T(8,128)S(1)}, s32[32,128]{1,0:T(8,128)}, u32[]{:S(2)}) copy-start(s32[32,128]{1,0:T(8,128)} %wall.3) | copy-start | bytes 49156
  4.2 12.6 %copy-start.1 = (f32[3,128,32,128]{3,2,1,0:T(8,128)S(1)}, f32[3,128,32,128]{3,2,1,0:T(8,128)}, u32[]{:S(2)}) copy-start(f32[3,128,32,128]{3,2,1,0:T(8,128)} %param.10) | copy-start | bytes 18874372
  4.2 12.6 %copy-start.4 = (s32[32,128]{1,0:T(8,128)S(1)}, s32[32,128]{1,0:T(8,128)}, u32[]{:S(2)}) copy-start(s32[32,128]{1,0:T(8,128)} %hart.1) | copy-start | bytes 49156
  16.9 0.9 %copy-start.2 = (bf16[256,256]{1,0:T(8,128)(2,1)S(1)}, bf16[256,256]{1,0:T(8,128)(2,1)}, u32[]{:S(2)}) copy-start(bf16[256,256]{1,0:T(8,128)(2,1)} %w_mid.1) | copy-start | bytes 393220
  17.8 0.7 %copy-start.5 = (bf16[256,24]{0,1:T(8,128)(2,1)S(1)}, bf16[256,24]{0,1:T(8,128)(2,1)}, u32[]{:S(2)}) copy-start(bf16[256,24]{0,1:T(8,128)(2,1)} %param.14) | copy-start | bytes 36868
  18.5 0.7 %copy-start.6 = (s32[8,2,8]{2,1,0:T(2,128)S(1)}, s32[8,2,8]{2,1,0:T(2,128)}, u32[]{:S(2)}) copy-start(s32[8,2,8]{2,1,0:T(2,128)} %table.1) | copy-start | bytes 1540

commit v3 on v2

v3 whole, which is shorter than its diff:
```python
import functools

import jax
import jax.numpy as jnp
from jax import lax
from jax.experimental import pallas as pl
from jax.experimental.pallas import tpu as pltpu
from jax.sharding import PartitionSpec as P

MESH = pl.DeviceIdType.MESH
STATIONS = 128
CY = 32
CZ = 128
HID = 256
N_GY = 16
N_GZ = 8
TILES = 128
SAMPLES = 1048576
ROWS = 3 * STATIONS * CY
SLABS = 8
VMEM_LIMIT = 56
MOVES = 8
LANES = 1024
F32 = jnp.float32
BF16 = jnp.bfloat16
PAIRS = ((0, 0), (1, 1), (2, 2), (0, 1), (0, 2), (1, 2))
NT = (((1,), (1,)), ((), ()))


def iota(shape, dim):
    return lax.broadcasted_iota(jnp.int32, shape, dim)


def wait_bytes(ref, sem):
    pltpu.make_async_copy(ref, ref, sem).wait()


def column_table(row):
    wide = jnp.broadcast_to(row, (128, HID))
    return jnp.concatenate([jnp.transpose(wide[:, :128]), jnp.transpose(wide[:, 128:])], axis=0)


def prepare_weights(w_in, b_in, w_mid, b_mid, w_out, b_out, win, wmid, wmid_t, wout, wout_t, bias_mid, bias_out, tmp):
    lane = iota((HID, 128), 1)
    bias = column_table(b_in[...]) * 0.5
    high = bias.astype(BF16).astype(F32)
    tmp[pl.ds(0, 128), :] = jnp.zeros((128, 128), F32)
    halves = []
    for h in range(2):
        tmp[pl.ds(0, 24), :] = w_in[:, 128 * h : 128 * h + 128].astype(F32) * 0.5
        halves.append(jnp.transpose(tmp[pl.ds(0, 128), :]))
    full = jnp.concatenate(halves, axis=0)
    full = jnp.where(lane == 30, high, jnp.where(lane == 31, bias - high, full))
    win[...] = full[:, 0:32].astype(BF16)
    mid = w_mid[...].astype(F32) * 0.5
    wmid[...] = mid.astype(BF16)
    wmid_t[...] = jnp.transpose(mid).astype(BF16)
    bias_mid[...] = column_table(b_mid[...]) * 0.5
    for h in range(2):
        tmp[pl.ds(0, 128), :] = jnp.zeros((128, 128), F32)
        tmp[pl.ds(0, 6), :] = w_out[:, 128 * h : 128 * h + 128].astype(F32)
        wout[:, 128 * h : 128 * h + 128] = tmp[pl.ds(0, 16), :].astype(BF16)
        wout_t[pl.ds(128 * h, 128), :] = (jnp.transpose(tmp[pl.ds(0, 128), :])[:, 0:16] * 0.5).astype(BF16)
    row = iota((8, 128), 0)
    table = jnp.where(row >= 6, 1.0, 0.0)
    tmp[pl.ds(0, 1), 0:6] = b_out[...]
    wide = jnp.broadcast_to(tmp[pl.ds(0, 1), :], (128, 128))
    bias_out[...] = jnp.where(row < 6, jnp.transpose(wide)[0:8], table)


def pack_edges(v, fluid, edge_lo, edge_hi, c):
    first = c * STATIONS * CY
    rows = pl.ds(c * STATIONS, STATIONS)
    edge_lo[rows, :] = (v[pl.ds(first, STATIONS, stride=CY), :] * fluid[0:1, :]).astype(BF16)
    edge_hi[rows, :] = (v[pl.ds(first + CY - 1, STATIONS, stride=CY), :] * fluid[CY - 1 : CY, :]).astype(BF16)


def pack_columns(v, fluid, to_left, to_right, c):
    pair = iota((8, 128), 1) // 2
    odd = iota((8, 128), 1) % 2 == 1
    def station(s, acc):
        here = pair == s
        out = []
        for h in range(2):
            for j in range(4):
                cells = v[pl.ds((c * STATIONS + h * 64 + s) * CY + 8 * j, 8), :]
                out.append(jnp.where(here, pltpu.roll(cells, 2 * s + 1, 1), acc[len(out)]))
        return tuple(out)

    packed = lax.fori_loop(0, 64, station, tuple(jnp.zeros((8, 128), F32) for _ in range(8)), unroll=8)
    for k in range(2):
        left, right = [], []
        for j in (2 * k, 2 * k + 1):
            mask = fluid[8 * j : 8 * j + 8, :]
            near, far = packed[j], packed[4 + j]
            right.append(jnp.where(odd, pltpu.roll(far, 1, 1), near) * mask[:, CZ - 1 : CZ])
            left.append(jnp.where(odd, far, pltpu.roll(near, 127, 1)) * mask[:, 0:1])
        rows = pl.ds(c * CY + 16 * k, 16)
        to_right[rows, :] = jnp.concatenate(right, axis=0).astype(BF16)
        to_left[rows, :] = jnp.concatenate(left, axis=0).astype(BF16)


def stencil_station(v, lo, hi, col, tables, stepped, rounded, st, s):
    ahead = lax.rem(st + 1, STATIONS)
    behind = lax.rem(st + STATIONS - 1, STATIONS)
    half = st // 64
    shift = 126 - 2 * lax.rem(st, 64)
    first_row = iota((8, 128), 0) == 0
    last_row = iota((8, 128), 0) == 7
    first_lane = iota((8, 128), 1) == 0
    last_lane = iota((8, 128), 1) == CZ - 1

    def cells(c, t, j):
        return v[pl.ds((c * STATIONS + t) * CY + 8 * j, 8), :]

    m = [[cells(c, st, j) * tables[pl.ds(8 * j, 8), :] for j in range(4)] for c in range(3)]
    minus = [[1.0 - m[c][j] for j in range(4)] for c in range(3)]
    plus = [[1.0 + m[c][j] for j in range(4)] for c in range(3)]
    for c in range(3):
        edge_lo = jnp.broadcast_to(lo[pl.ds(c * STATIONS + st, 1), :], (8, 128))
        edge_hi = jnp.broadcast_to(hi[pl.ds(c * STATIONS + st, 1), :], (8, 128))
        down = [edge_lo] + [pltpu.roll(m[c][j], 1, 0) for j in range(4)]
        up = [pltpu.roll(m[c][j], 7, 0) for j in range(4)] + [edge_hi]
        results = []
        for j in range(4):
            south = jnp.where(first_row, down[j], down[j + 1])
            north = jnp.where(last_row, up[j + 1], up[j])
            ends = pltpu.roll(col[pl.ds((c * 2 + half) * CY + 8 * j, 8), :], shift, 1)
            lower = jnp.where(first_lane, ends, pltpu.roll(m[c][j], 1, 1))
            upper = jnp.where(last_lane, ends, pltpu.roll(m[c][j], CZ - 1, 1))
            total = minus[0][j] * cells(c, ahead, j) + plus[0][j] * cells(c, behind, j)
            total = total + (minus[1][j] * north + plus[1][j] * south)
            total = total + (minus[2][j] * upper + plus[2][j] * lower)
            own = tables[pl.ds(64 + 8 * j, 8), :] if c < 2 else 4.0
            total = total + own * m[c][j]
            results.append(total * tables[pl.ds(32 + 8 * j, 8), :])
        for k in range(2):
            value = jnp.concatenate(results[2 * k : 2 * k + 2], axis=0).astype(BF16)
            stepped[pl.ds(pl.multiple_of((c * STATIONS + st) * CY + 16 * k, 16), 16), :] = value
            rounded[pl.ds((c * 16 + s) * CY + 16 * k, 16), :] = value.astype(F32)


def pool_slab(rounded, feat):
    residue = iota((8, 128), 1) % 4
    merged = [None] * 30

    def put(f, r, value, source):
        shift = (r - source) % 128
        value = pltpu.roll(value, shift, 1) if shift else value
        merged[f] = value if merged[f] is None else jnp.where(residue == r, value, merged[f])

    for r in range(4):
        sums = [[None] * 4 for _ in range(3)]
        products = [None] * 6
        for dx in range(4):
            for dy in range(4):
                q = (dx // 2) * 2 + dy // 2
                u = [rounded[pl.ds((c * 16 + 4 * r + dx) * CY + dy, 8, stride=4), :] for c in range(3)]
                for c in range(3):
                    sums[c][q] = u[c] if sums[c][q] is None else sums[c][q] + u[c]
                for k, (a, b) in enumerate(PAIRS):
                    value = u[a] * u[b]
                    products[k] = value if products[k] is None else products[k] + value
        means = []
        for c in range(3):
            point = None
            for q in range(4):
                two = sums[c][q] + pltpu.roll(sums[c][q], 127, 1)
                put(c * 8 + 2 * q, r, two, 0)
                put(c * 8 + 2 * q + 1, r, two, 2)
                point = two if point is None else point + two
            means.append((point + pltpu.roll(point, 126, 1)) * (1.0 / 64))
        for k, (a, b) in enumerate(PAIRS):
            two = products[k] + pltpu.roll(products[k], 127, 1)
            four = two + pltpu.roll(two, 126, 1)
            put(24 + k, r, four * (1.0 / 64) - means[a] * means[b], 0)
    for f in range(24):
        feat[pl.ds(8 * f, 8), :] = merged[f] * 0.125
    for f in range(24, 30):
        feat[pl.ds(8 * f, 8), :] = merged[f].astype(BF16).astype(F32)


def widen(table, lanes):
    return jnp.concatenate([table] * (lanes // 128), axis=1)


def lane_sum(value):
    total = value[:, 0:128]
    for k in range(1, value.shape[1] // 128):
        total = total + value[:, 128 * k : 128 * k + 128]
    return total


def train_part(x, targets, win, wmid, wmid_t, wout, wout_t, bias_mid, bias_out, pred, g_in, g_mid, g_out, g_bmid, g_bout, g_loss):
    n = x.shape[1]
    h1 = jnp.dot(win[...], x, preferred_element_type=F32)
    t1 = jnp.tanh(h1)
    p1 = 1.0 + t1
    a1 = h1 * p1
    slope1 = p1 + a1 * (2.0 - p1)
    act1 = a1.astype(BF16)
    h2 = jnp.dot(wmid[...], act1, preferred_element_type=F32) + widen(bias_mid[...], n)
    p2 = 1.0 + jnp.tanh(h2)
    a2 = h2 * p2
    slope2 = p2 + a2 * (2.0 - p2)
    act2 = a2.astype(BF16)
    prediction = jnp.dot(wout[...], act2, preferred_element_type=F32)[0:8] + widen(bias_out[...], n)
    pred[...] = prediction
    residual = prediction - targets
    g_loss[...] += lane_sum(residual * residual)
    grad = (residual * (2.0 / (6 * SAMPLES))).astype(BF16).astype(F32)
    g_bout[...] += lane_sum(grad)
    grad = jnp.concatenate([grad, jnp.zeros_like(grad)], axis=0).astype(BF16)
    g_out[...] += lax.dot_general(grad, act2, NT, preferred_element_type=F32)
    d2 = jnp.dot(wout_t[...], grad, preferred_element_type=F32) * slope2
    g_bmid[...] += lane_sum(d2)
    grad2 = d2.astype(BF16)
    g_mid[...] += lax.dot_general(grad2, act1, NT, preferred_element_type=F32)
    d1 = jnp.dot(wmid_t[...], grad2, preferred_element_type=F32) * slope1
    grad1 = d1.astype(BF16)
    g_in[...] += lax.dot_general(grad1, x, NT, preferred_element_type=F32)


def keep_predictions(a, pred, tiles):
    lane = iota((8, 128), 1)
    point = lane % 64
    quarter = point // 4 % 4
    source = 4 * (point % 4) + point // 16
    low = lane < 64
    for b in range(2):
        blocks = [pred[:, 128 * (4 * b + q) : 128 * (4 * b + q) + 128] for q in range(4)]
        for c in range(8):
            index = source + 16 * c
            value = jnp.take_along_axis(blocks[0], index, axis=1)
            for q in range(1, 4):
                value = jnp.where(quarter == q, jnp.take_along_axis(blocks[q], index, axis=1), value)
            value = jnp.where(low, value, pltpu.roll(value, 5, 0))
            for k in range(3):
                tiles[pl.ds(k * TILES + a * 16 + b * 8 + c, 1), :] = value[k : k + 1]


def order_tiles(table, row, tiles, ordered):
    for a in range(8):
        for b in range(2):
            first = a * 16 + b * 8
            row[0:1, first : first + 8] = table[a, b : b + 1, :]
    place = iota((TILES, 128), 0)
    slot = place % N_GY * N_GZ + place // N_GY
    chosen = jnp.where(jnp.broadcast_to(row[0:1, :], (TILES, 128)) == slot, 1.0, 0.0).astype(BF16)
    for k in range(3):
        value = tiles[pl.ds(k * TILES, TILES), :]
        high = value.astype(BF16)
        rest = value - high.astype(F32)
        middle = rest.astype(BF16)
        last = (rest - middle.astype(F32)).astype(BF16)
        total = jnp.dot(chosen, high, preferred_element_type=F32)
        total = total + jnp.dot(chosen, middle, preferred_element_type=F32)
        total = total + jnp.dot(chosen, last, preferred_element_type=F32)
        ordered[:, k, :] = total


def pack_gradients(g_in, g_mid, g_out, g_bmid, g_bout, g_loss, tmp, grads):
    for t in range(64):
        grads[t // 5, t % 5] = g_mid[pl.ds(8 * (t // 2), 8), 128 * (t % 2) : 128 * (t % 2) + 128]
    tmp[:, 0:32] = g_in[...]
    for h in range(2):
        turned = jnp.transpose(tmp[pl.ds(128 * h, 128), :])
        for k in range(4):
            t = 64 + 2 * k + h
            grads[t // 5, t % 5] = turned[8 * k : 8 * k + 8]
    row = iota((8, 128), 0)
    lane = iota((8, 128), 1)
    sums_out = jnp.sum(g_bout[...], axis=1, keepdims=True)
    last = jnp.sum(jnp.where((lane == row + 8) & (row < 6), sums_out, 0.0), axis=0, keepdims=True)
    loss = jnp.sum(jnp.sum(g_loss[...], axis=1, keepdims=True), axis=0, keepdims=True)
    last = jnp.where(lane[0:1] == 0, loss, last)
    for k in range(2):
        t = 72 + k
        bias = jnp.sum(jnp.transpose(g_bmid[pl.ds(128 * k, 128), :]), axis=0, keepdims=True)
        value = g_out[pl.ds(0, 8), 128 * k : 128 * k + 128]
        grads[t // 5, t % 5] = jnp.where(row == 6, bias, jnp.where(row == 7, last, value))
    for t in range(74, 80):
        grads[t // 5, t % 5] = jnp.zeros((8, 128), F32)


def whole_kernel(
    vel, wall_any, hart_any, table_any, w_in_any, b_in_any, w_mid_any, b_mid_any, w_out_any, b_out_any,
    stepped_out, total, got,
    v, wall, hart, table, w_in, b_in, w_mid, b_mid, w_out, b_out,
    win, wmid, wmid_t, wout, wout_t, bias_mid, bias_out, tmp, row,
    edge_lo, edge_hi, to_left, to_right, got_lo, got_hi, got_left, got_right, lo, hi, col,
    stepped, rounded, tables, feat, xs, targets, pred, tiles, ordered,
    g_in, g_mid, g_out, g_bmid, g_bout, g_loss, grads, part, mine, column, hop,
    load, send_halo, recv_halo, store, s0, r0, s1, r1, s2, r2, s3, r3, s4, r4,
):
    y = lax.axis_index("gy")
    z = lax.axis_index("gz")
    slabs = [pl.ds(c * STATIONS * CY, STATIONS * CY) for c in range(3)]
    loads = [pltpu.make_async_copy(wall_any, wall, load.at[0])]
    loads += [pltpu.make_async_copy(vel.at[slabs[c]], v.at[slabs[c]], load.at[1 + c]) for c in range(3)]
    pairs = (
        (w_in_any, w_in), (b_in_any, b_in), (w_mid_any, w_mid), (b_mid_any, b_mid),
        (w_out_any, w_out), (b_out_any, b_out), (hart_any, hart), (table_any, table),
    )
    loads += [pltpu.make_async_copy(src, dst, load.at[4 + k]) for k, (src, dst) in enumerate(pairs)]
    for copy in loads:
        copy.start()

    barrier = pltpu.get_barrier_semaphore()
    for d in range(1, N_GY):
        pl.semaphore_signal(barrier, inc=1, device_id=((y + d) % N_GY, z), device_id_type=MESH)
    for d in range(1, N_GZ):
        pl.semaphore_signal(barrier, inc=1, device_id=(y, (z + d) % N_GZ), device_id_type=MESH)

    loads[0].wait()
    fluid = (1 - wall[...]).astype(F32)
    tables[pl.ds(0, 32), :] = fluid
    tables[pl.ds(32, 32), :] = fluid * 0.1
    for c in range(3):
        loads[1 + c].wait()
        pack_columns(v, tables, to_left, to_right, c)
        pack_edges(v, tables, edge_lo, edge_hi, c)
    pl.semaphore_wait(barrier, N_GY + N_GZ - 2)
    below = ((y + N_GY - 1) % N_GY, z)
    above = ((y + 1) % N_GY, z)
    left = (y, (z + N_GZ - 1) % N_GZ)
    right = (y, (z + 1) % N_GZ)
    copies = []
    for k, (src, dst, peer) in enumerate(
        ((to_left, got_right, left), (to_right, got_left, right), (edge_lo, got_hi, below), (edge_hi, got_lo, above))
    ):
        copy = pltpu.make_async_remote_copy(
            src, dst, send_halo.at[k], recv_halo.at[k], device_id=peer, device_id_type=MESH
        )
        copy.start()
        copies.append(copy)
    for copy in loads[4:]:
        copy.wait()
    tables[pl.ds(64, 32), :] = 2.0 - 2.0 * hart[...].astype(F32)
    prepare_weights(w_in, b_in, w_mid, b_mid, w_out, b_out, win, wmid, wmid_t, wout, wout_t, bias_mid, bias_out, tmp)
    for ref in (g_in, g_mid, g_out, g_bmid, g_bout, g_loss):
        ref[...] = jnp.zeros_like(ref)
    feat[pl.ds(240, 16), :] = jnp.ones((16, 128), F32)
    for copy in copies:
        copy.wait_recv()
    lo[...] = got_lo[...].astype(F32) * jnp.where(y > 0, 1.0, 0.0)
    hi[...] = got_hi[...].astype(F32) * jnp.where(y < N_GY - 1, 1.0, 0.0)
    has_left = jnp.where(z > 0, 1.0, 0.0)
    has_right = jnp.where(z < N_GZ - 1, 1.0, 0.0)
    odd = iota((16, 128), 1) % 2 == 1
    for c in range(3):
        for k in range(2):
            rows = pl.ds(c * CY + 16 * k, 16)
            lower = got_left[rows, :].astype(F32) * has_left
            upper = got_right[rows, :].astype(F32) * has_right
            near = jnp.where(odd, pltpu.roll(upper, 1, 1), pltpu.roll(lower, 2, 1))
            far = jnp.where(odd, upper, pltpu.roll(lower, 1, 1))
            col[pl.ds((c * 2) * CY + 16 * k, 16), :] = near
            col[pl.ds((c * 2 + 1) * CY + 16 * k, 16), :] = far

    def store_copy(c, a):
        rows = pl.ds(pl.multiple_of(c * STATIONS * CY + a * 16 * CY, 16), 16 * CY)
        return pltpu.make_async_copy(stepped.at[rows], stepped_out.at[rows], store.at[c])

    def stencil_slab(a, unroll):
        def station(s, inner):
            stencil_station(v, lo, hi, col, tables, stepped, rounded, a * 16 + s, s)
            return inner

        lax.fori_loop(0, 16, station, 0, unroll=unroll)
        for c in range(3):
            store_copy(c, a).start()

    def samples():
        pool_slab(rounded, feat)
        for yp in range(8):
            lanes = slice(128 * yp, 128 * yp + 128)
            xs[:, lanes] = feat[pl.ds(yp, 32, stride=8), :].astype(BF16)
            targets[:, lanes] = feat[pl.ds(192 + yp, 8, stride=8), :]

    def train(a):
        train_part(
            xs[...], targets[...], win, wmid, wmid_t, wout, wout_t, bias_mid, bias_out,
            pred, g_in, g_mid, g_out, g_bmid, g_bout, g_loss,
        )
        keep_predictions(a, pred, tiles)

    def slab(a, carry):
        samples()
        train(a)
        stencil_slab(a + 1, 16)
        return carry

    stencil_slab(0, 4)
    lax.fori_loop(0, SLABS - 1, slab, 0)
    samples()
    train(SLABS - 1)
    pack_gradients(g_in, g_mid, g_out, g_bmid, g_bout, g_loss, tmp, grads)

    def send(src, dst, ss, rs, qy, qz):
        pltpu.make_async_remote_copy(src, dst, ss, rs, device_id=(qy, qz), device_id_type=MESH).start()

    for d in range(1, N_GY):
        q = (y + d) % N_GY
        send(grads.at[q], part.at[y], s0, r0, q, z)
    order_tiles(table, row, tiles, ordered)
    for d in range(1, N_GZ):
        q = (z + d) % N_GZ
        send(ordered.at[pl.ds(q * N_GY, N_GY)], hop.at[z], s1, r1, y, q)
    hop[z] = ordered[pl.ds(z * N_GY, N_GY)]
    part[y] = grads[y]
    wait_bytes(part.at[pl.ds(0, N_GY - 1)], r0)
    column[z] = jnp.sum(part[...], axis=0)
    for d in range(1, N_GZ):
        q = (z + d) % N_GZ
        send(column.at[z], column.at[z], s2, r2, y, q)
    wait_bytes(hop.at[pl.ds(0, N_GZ - 1)], r1)
    for d in range(1, N_GY):
        q = (y + d) % N_GY
        send(hop.at[:, q], got.at[y], s3, r3, q, z)
    got[y] = hop[:, y]
    wait_bytes(column.at[pl.ds(0, N_GZ - 1)], r2)
    mine[...] = jnp.sum(column[...], axis=0)
    for d in range(1, N_GY):
        q = (y + d) % N_GY
        send(mine, total.at[y], s4, r4, q, z)
    total[y] = mine[...]
    for c in range(3):
        wait_bytes(stepped.at[slabs[c]], store.at[c])
    for copy in copies:
        copy.wait_send()
    wait_bytes(got.at[pl.ds(0, N_GY - 1)], r3)
    wait_bytes(total.at[pl.ds(0, N_GY - 1)], r4)
    wait_bytes(part.at[pl.ds(0, N_GY - 1)], s0)
    wait_bytes(hop.at[pl.ds(0, N_GZ - 1)], s1)
    wait_bytes(column.at[pl.ds(0, N_GZ - 1)], s2)
    wait_bytes(got.at[pl.ds(0, N_GY - 1)], s3)
    wait_bytes(total.at[pl.ds(0, N_GY - 1)], s4)


def whole_call(*arrays):
    vm = pl.BlockSpec(memory_space=pltpu.VMEM)
    anywhere = pl.BlockSpec(memory_space=pl.ANY)
    i32 = jnp.int32
    scratch = [
        ((ROWS, 128), F32), ((CY, 128), i32), ((CY, 128), i32), ((8, 2, 8), i32), ((24, HID), BF16), ((1, HID), F32),
        ((HID, HID), BF16), ((1, HID), F32), ((6, HID), BF16), ((1, 6), F32),
        ((HID, 32), BF16), ((HID, HID), BF16), ((HID, HID), BF16), ((16, HID), BF16), ((HID, 16), BF16),
        ((HID, 128), F32), ((8, 128), F32), ((HID, 128), F32), ((8, 128), i32),
        ((384, 128), BF16), ((384, 128), BF16), ((96, 128), BF16), ((96, 128), BF16),
        ((384, 128), BF16), ((384, 128), BF16), ((96, 128), BF16), ((96, 128), BF16),
        ((384, 128), F32), ((384, 128), F32), ((192, 128), F32),
        ((ROWS, 128), BF16), ((3 * 16 * CY, 128), F32), ((96, 128), F32), ((256, 128), F32),
        ((32, LANES), BF16), ((8, LANES), F32), ((8, LANES), F32), ((3 * TILES, 128), F32), ((TILES, 3, 128), F32),
        ((HID, 32), F32), ((HID, HID), F32), ((16, HID), F32), ((HID, 128), F32), ((8, 128), F32), ((8, 128), F32),
        ((N_GY, 5, 8, 128), F32), ((N_GY, 5, 8, 128), F32), ((5, 8, 128), F32), ((N_GZ, 5, 8, 128), F32),
        ((N_GZ, N_GY, 3, 128), F32),
    ]
    dma = pltpu.SemaphoreType.DMA
    return pl.pallas_call(
        whole_kernel,
        name="whole",
        out_shape=[
            jax.ShapeDtypeStruct((ROWS, 128), BF16),
            jax.ShapeDtypeStruct((N_GY, 5, 8, 128), F32),
            jax.ShapeDtypeStruct((N_GY, N_GZ, 3, 128), F32),
        ],
        in_specs=[anywhere] * 10,
        out_specs=[anywhere, vm, vm],
        scratch_shapes=[pltpu.VMEM(shape, kind) for shape, kind in scratch] + [dma((12,)), dma((4,)), dma((4,)), dma((3,))] + [dma] * 10,
        compiler_params=pltpu.CompilerParams(collective_id=0, has_side_effects=True, vmem_limit_bytes=VMEM_LIMIT << 20),
    )(*arrays)


def finish_kernel(
    stepped_any, total_any, got_any,
    stepped_out, pred_out, loss_out, in_out, bin_out, mid_out, bmid_out, out_out, bout_out,
    held, total, got, load, take, give,
):
    fetch_got = pltpu.make_async_copy(got_any, got, load.at[0])
    fetch_total = pltpu.make_async_copy(total_any, total, load.at[1])
    fetch_got.start()
    fetch_total.start()
    count = ROWS // MOVES
    parts = [pl.ds(k * count, count) for k in range(MOVES)]
    takes = [pltpu.make_async_copy(stepped_any.at[parts[k]], held.at[parts[k]], take.at[k]) for k in range(MOVES)]
    gives = [pltpu.make_async_copy(held.at[parts[k]], stepped_out.at[parts[k]], give.at[k]) for k in range(MOVES)]
    for copy in takes:
        copy.start()
    for k in range(MOVES):
        takes[k].wait()
        gives[k].start()
    fetch_got.wait()
    low = iota((3, 128), 1) < 64
    for j in range(TILES // 2):
        first = got[(2 * j) // N_GZ, (2 * j) % N_GZ]
        second = got[(2 * j + 1) // N_GZ, (2 * j + 1) % N_GZ]
        lanes = slice(128 * j, 128 * j + 128)
        pred_out[0:3, lanes] = jnp.where(low, first, pltpu.roll(second, 64, 1))
        pred_out[3:6, lanes] = jnp.where(low, pltpu.roll(first, 64, 1), second)
    fetch_total.wait()
    for t in range(64):
        mid_out[pl.ds(8 * (t // 2), 8), 128 * (t % 2) : 128 * (t % 2) + 128] = total[t // 5, t % 5]
    for h in range(2):
        lanes = slice(128 * h, 128 * h + 128)
        for k in range(4):
            t = 64 + 2 * k + h
            if k < 3:
                in_out[pl.ds(8 * k, 8), lanes] = total[t // 5, t % 5]
            else:
                bin_out[:, lanes] = total[t // 5, t % 5][6:7]
        last = total[(72 + h) // 5, (72 + h) % 5]
        out_out[:, lanes] = last[0:6]
        bmid_out[:, lanes] = last[6:7]
        if h == 0:
            loss_out[...] = last[7:8, 0:1] * (1.0 / (6 * SAMPLES))
            bout_out[...] = pltpu.roll(last, 120, 1)[7:8, 0:6]
    for copy in gives:
        copy.wait()


def finish_call(stepped, total, got):
    anywhere = pl.BlockSpec(memory_space=pl.ANY)
    vm = pl.BlockSpec(memory_space=pltpu.VMEM)
    return pl.pallas_call(
        finish_kernel,
        name="finish",
        out_shape=[
            jax.ShapeDtypeStruct((ROWS, 128), BF16),
            jax.ShapeDtypeStruct((6, 64 * 128), F32),
            jax.ShapeDtypeStruct((1, 1), F32),
            jax.ShapeDtypeStruct((24, HID), F32),
            jax.ShapeDtypeStruct((1, HID), F32),
            jax.ShapeDtypeStruct((HID, HID), F32),
            jax.ShapeDtypeStruct((1, HID), F32),
            jax.ShapeDtypeStruct((6, HID), F32),
            jax.ShapeDtypeStruct((1, 6), F32),
        ],
        in_specs=[anywhere] * 3,
        out_specs=[anywhere] + [vm] * 8,
        scratch_shapes=[
            pltpu.VMEM((ROWS, 128), BF16),
            pltpu.VMEM((N_GY, 5, 8, 128), F32),
            pltpu.VMEM((N_GY, N_GZ, 3, 128), F32),
            pltpu.SemaphoreType.DMA((2,)),
            pltpu.SemaphoreType.DMA((MOVES,)),
            pltpu.SemaphoreType.DMA((MOVES,)),
        ],
        compiler_params=pltpu.CompilerParams(vmem_limit_bytes=VMEM_LIMIT << 20),
    )(stepped, total, got)


def on_device(velocity, wall_mask, hartmann_mask, tile_table, w_in, b_in, w_mid, b_mid, w_out, b_out):
    stepped, total, got = whole_call(
        velocity.reshape(ROWS, CZ), wall_mask, hartmann_mask, tile_table,
        w_in.T, b_in.reshape(1, HID), w_mid, b_mid.reshape(1, HID), w_out, b_out.reshape(1, 6),
    )
    stepped, prediction, loss, grad_in, grad_bin, grad_mid, grad_bmid, grad_out, grad_bout = finish_call(stepped, total, got)
    return (
        stepped.reshape(3, STATIONS, CY, CZ),
        prediction,
        loss.reshape(()),
        grad_in.T,
        grad_bin.reshape(HID),
        grad_mid,
        grad_bmid.reshape(HID),
        grad_out,
        grad_bout.reshape(6),
    )


def solution(mesh):
    whole = P()
    in_specs = (P(None, None, "gy", "gz"), P("gy", "gz"), P("gy", "gz"), P(None, "gy", "gz")) + (whole,) * 6
    out_specs = (P(None, None, "gy", "gz"), P(None, ("gy", "gz"))) + (whole,) * 7
    return jax.shard_map(on_device, mesh=mesh, in_specs=in_specs, out_specs=out_specs, check_vma=False)
```

time: 62.1 us -> 57.7 us (0.929)
  local copies, waits for them, and re-layouts: 5.84 us -> 0 us
  Pallas kernels: 55.2 us -> 56.8 us
    unnamed x22 -> x0, local copies, waits for them, and re-layouts: 5.84 us -> none
    pallas_call x1, Pallas kernels: 0.95 us -> 3.92 us  [finish_call(): pl.pallas_call(finish_kernel, name='finish', out_shape=[jax.ShapeDtypeStr...]
    pallas_call x3 -> x1, Pallas kernels: 54.2 us -> 52.9 us  [whole_call(): pl.pallas_call(whole_kernel, name='whole', out_shape=[jax.ShapeDtypeStruc...]
where the time goes in v3:
time: 57.7 us; the launch traced here: 57.5 us
  Pallas kernels  56.8 us (98%)
  between operations  0.65 us (1%)
    pallas_call x1, Pallas kernels, whole_call(): pl.pallas_call(whole_kernel, name='whole', out_shape=[jax.ShapeDtypeStruc...  52.9 us
    pallas_call x1, Pallas kernels, finish_call(): pl.pallas_call(finish_kernel, name='finish', out_shape=[jax.ShapeDtypeStr...  3.92 us

profile of v3, /device:TPU:1, one launch (start us, length us, event | category | flops | bytes accessed | tf_op | source)
XLA Modules:
  0.0 57.5 jit_solution(15386661956384533131)
XLA Ops:
  0.6 52.9 %whole.1 = (bf16[12288,128]{1,0:T(8,128)(2,1)}, f32[16,5,8,128]{3,2,1,0:T(8,128)}, f32[16,8,3,128]{3,2,1,0:T(4,128)}) custom-call(f32[12288,128]{1,0:T(8,128)} %bitcast.11, s32[32,128]{1,0:T(8,128)} %wall_any.1, s32[32,128]{1,0:T(8,128)} %hart_any.1, s32[8,2,8]{2,1,0:T(2,128)} %table_any.1, bf16[24,256]{1,0:T(8,128)(2,1)} %bitcast.12, f32[1,256]{1,0:T(1,128)} %bitcast.13, ...), custom_call_target="tpu_custom_call" | custom-call | tf_op jit(solution)/shard_map/whole/pallas_call | solution.py:460
  53.6 3.9 %finish.1 = (bf16[12288,128]{1,0:T(8,128)(2,1)}, f32[6,8192]{1,0:T(8,128)}, f32[1,1]{1,0:T(1,128)}, f32[24,256]{1,0:T(8,128)}, f32[1,256]{1,0:T(1,128)}, /*index...) custom-call(bf16[12288,128]{1,0:T(8,128)(2,1)} %get-tuple-element.21.stepped_any, ...), custom_call_target="tpu_custom_call" | custom-call | tf_op jit(solution)/shard_map/finish/pallas_call | solution.py:525

commit v4 on v3

--- a/solution.py
+++ b/solution.py
@@ -19,7 +19,7 @@
 ROWS = 3 * STATIONS * CY
 SLABS = 8
 VMEM_LIMIT = 56
-MOVES = 8
+MOVES = 4
 LANES = 1024
 F32 = jnp.float32
 BF16 = jnp.bfloat16
@@ -87,7 +87,7 @@
                 out.append(jnp.where(here, pltpu.roll(cells, 2 * s + 1, 1), acc[len(out)]))
         return tuple(out)
 
-    packed = lax.fori_loop(0, 64, station, tuple(jnp.zeros((8, 128), F32) for _ in range(8)), unroll=8)
+    packed = lax.fori_loop(0, 64, station, tuple(jnp.zeros((8, 128), F32) for _ in range(8)), unroll=64)
     for k in range(2):
         left, right = [], []
         for j in (2 * k, 2 * k + 1):
@@ -391,7 +391,7 @@
         stencil_slab(a + 1, 16)
         return carry
 
-    stencil_slab(0, 4)
+    stencil_slab(0, 16)
     lax.fori_loop(0, SLABS - 1, slab, 0)
     samples()
     train(SLABS - 1)

time: 57.7 us -> 56.1 us (0.972)
  Pallas kernels: 56.8 us -> 55.3 us
    pallas_call x1, Pallas kernels: 52.9 us -> 51.5 us  [whole_call(): pl.pallas_call(whole_kernel, name='whole', out_shape=[jax.ShapeDtypeStruc...]
where the time goes in v4:
time: 56.1 us; the launch traced here: 55.9 us
  Pallas kernels  55.3 us (99%)
  between operations  0.65 us (1%)
    pallas_call x1, Pallas kernels, whole_call(): pl.pallas_call(whole_kernel, name='whole', out_shape=[jax.ShapeDtypeStruc...  51.5 us
    pallas_call x1, Pallas kernels, finish_call(): pl.pallas_call(finish_kernel, name='finish', out_shape=[jax.ShapeDtypeStr...  3.78 us

profile of v4, /device:TPU:1, one launch (start us, length us, event | category | flops | bytes accessed | tf_op | source)
XLA Modules:
  0.0 55.9 jit_solution(16790171717604742853)
XLA Ops:
  0.6 51.5 %whole.1 = (bf16[12288,128]{1,0:T(8,128)(2,1)}, f32[16,5,8,128]{3,2,1,0:T(8,128)}, f32[16,8,3,128]{3,2,1,0:T(4,128)}) custom-call(f32[12288,128]{1,0:T(8,128)} %bitcast.11, s32[32,128]{1,0:T(8,128)} %wall_any.1, s32[32,128]{1,0:T(8,128)} %hart_any.1, s32[8,2,8]{2,1,0:T(2,128)} %table_any.1, bf16[24,256]{1,0:T(8,128)(2,1)} %bitcast.12, f32[1,256]{1,0:T(1,128)} %bitcast.13, ...), custom_call_target="tpu_custom_call" | custom-call | tf_op jit(solution)/shard_map/whole/pallas_call | solution.py:460
  52.1 3.8 %finish.1 = (bf16[12288,128]{1,0:T(8,128)(2,1)}, f32[6,8192]{1,0:T(8,128)}, f32[1,1]{1,0:T(1,128)}, f32[24,256]{1,0:T(8,128)}, f32[1,256]{1,0:T(1,128)}, /*index...) custom-call(bf16[12288,128]{1,0:T(8,128)(2,1)} %get-tuple-element.21.stepped_any, ...), custom_call_target="tpu_custom_call" | custom-call | tf_op jit(solution)/shard_map/finish/pallas_call | solution.py:525

commit v5 on v4

--- a/solution.py
+++ b/solution.py
@@ -19,6 +19,8 @@
 ROWS = 3 * STATIONS * CY
 SLABS = 8
 VMEM_LIMIT = 56
+FAR_GY = (8, 7, 9, 6, 10, 5, 11, 4, 12, 3, 13, 2, 14, 1, 15)
+FAR_GZ = (4, 3, 5, 2, 6, 1, 7)
 MOVES = 4
 LANES = 1024
 F32 = jnp.float32
@@ -400,28 +402,28 @@
     def send(src, dst, ss, rs, qy, qz):
         pltpu.make_async_remote_copy(src, dst, ss, rs, device_id=(qy, qz), device_id_type=MESH).start()
 
-    for d in range(1, N_GY):
+    for d in FAR_GY:
         q = (y + d) % N_GY
         send(grads.at[q], part.at[y], s0, r0, q, z)
     order_tiles(table, row, tiles, ordered)
-    for d in range(1, N_GZ):
+    for d in FAR_GZ:
         q = (z + d) % N_GZ
         send(ordered.at[pl.ds(q * N_GY, N_GY)], hop.at[z], s1, r1, y, q)
     hop[z] = ordered[pl.ds(z * N_GY, N_GY)]
     part[y] = grads[y]
     wait_bytes(part.at[pl.ds(0, N_GY - 1)], r0)
     column[z] = jnp.sum(part[...], axis=0)
-    for d in range(1, N_GZ):
+    for d in FAR_GZ:
         q = (z + d) % N_GZ
         send(column.at[z], column.at[z], s2, r2, y, q)
     wait_bytes(hop.at[pl.ds(0, N_GZ - 1)], r1)
-    for d in range(1, N_GY):
+    for d in FAR_GY:
         q = (y + d) % N_GY
         send(hop.at[:, q], got.at[y], s3, r3, q, z)
     got[y] = hop[:, y]
     wait_bytes(column.at[pl.ds(0, N_GZ - 1)], r2)
     mine[...] = jnp.sum(column[...], axis=0)
-    for d in range(1, N_GY):
+    for d in FAR_GY:
         q = (y + d) % N_GY
         send(mine, total.at[y], s4, r4, q, z)
     total[y] = mine[...]

time: 56.1 us -> 55.9 us (level)
  no operation moved by 1% of the time
where the time goes in v5:
time: 55.9 us; the launch traced here: 55.7 us
  Pallas kernels  55 us (98%)
  between operations  0.65 us (1%)
    pallas_call x1, Pallas kernels, whole_call(): pl.pallas_call(whole_kernel, name='whole', out_shape=[jax.ShapeDtypeStruc...  51.2 us
    pallas_call x1, Pallas kernels, finish_call(): pl.pallas_call(finish_kernel, name='finish', out_shape=[jax.ShapeDtypeStr...  3.78 us

profile of v5, /device:TPU:1, one launch (start us, length us, event | category | flops | bytes accessed | tf_op | source)
XLA Modules:
  0.0 55.7 jit_solution(7605931540258621613)
XLA Ops:
  0.6 51.2 %whole.1 = (bf16[12288,128]{1,0:T(8,128)(2,1)}, f32[16,5,8,128]{3,2,1,0:T(8,128)}, f32[16,8,3,128]{3,2,1,0:T(4,128)}) custom-call(f32[12288,128]{1,0:T(8,128)} %bitcast.11, s32[32,128]{1,0:T(8,128)} %wall_any.1, s32[32,128]{1,0:T(8,128)} %hart_any.1, s32[8,2,8]{2,1,0:T(2,128)} %table_any.1, bf16[24,256]{1,0:T(8,128)(2,1)} %bitcast.12, f32[1,256]{1,0:T(1,128)} %bitcast.13, ...), custom_call_target="tpu_custom_call" | custom-call | tf_op jit(solution)/shard_map/whole/pallas_call | solution.py:462
  51.9 3.8 %finish.1 = (bf16[12288,128]{1,0:T(8,128)(2,1)}, f32[6,8192]{1,0:T(8,128)}, f32[1,1]{1,0:T(1,128)}, f32[24,256]{1,0:T(8,128)}, f32[1,256]{1,0:T(1,128)}, /*index...) custom-call(bf16[12288,128]{1,0:T(8,128)(2,1)} %get-tuple-element.21.stepped_any, ...), custom_call_target="tpu_custom_call" | custom-call | tf_op jit(solution)/shard_map/finish/pallas_call | solution.py:527
